TPU v7x, 256 devices: a whole 4x4x8 slice. The times are simulated.
256 devices in a mesh: comp: 2 (over core), aa: 8 (over z_hi, y), ba: 16 (over x, z_lo).
Axes of the slice: x: 4, y: 4, z: 8 (z_hi: 2, z_lo: 4; z = z_hi * 4 + z_lo), core: 2. Of those that a mesh axis runs over, the one named last changes fastest.
Arguments:
- legendre: bfloat16 [640, 32, 1280], P('aa'), may hold values from -0.15625 to 0.15625
- coefficients: bfloat16 [2, 640, 2, 64, 1280], P('comp', 'aa', None, 'ba'), may hold values from -0.1796875 to 0.1796875
- cycle_points: int32 [32], replicated, may hold values from 1024 to 4096, as said below
- spectra: float32 [128, 512, 1296], P('aa', 'ba', 'comp'), may hold values from 0.05 to 2
- sea_mask: int32 [128, 512], P('aa', 'ba'), may hold values 0 or 1
- wind_column: int32 [128, 512], P('aa'), may hold values from 0 to 4095, as said below
- roughness_source: int32 [32, 4096], P('aa', 'ba'), may hold values from 0 to 8191, as said below
Outputs:
- grid_winds: bfloat16 [2, 32, 64, 4096], P('comp', 'aa', None, 'ba')
- wave_spectra: float32 [128, 512, 1296], P('aa', 'ba', 'comp')
- charnock: float32 [32, 4096], P('aa', 'ba')
Inputs may be any that keep to these rules, and one draw needn't show every extreme that they name: `cycle_points`: at least a quarter of 4096; one cycle has exactly 4096 points. `wind_column`: each value is below the point count of cycle row // 4. `roughness_source`: the row within the band is one of the 4 rows (l mod 4) * 4 onward.
All inputs are finite; a program needn't handle non-finite values. No bound on the sum of `sea_mask` on one device may be relied on, other than what follows from the above.
Results may differ from a plain program's by a relative error of at most 0.0046.
The roundings to bfloat16 on the way count: a program that leaves them out, or rounds other values in their place, can miss the bound.
Values may be sent and summed in bfloat16 or wider, within the bound.
A program may use at most 64 MiB of HBM per device.

v0:
```python
import math

import jax
import jax.numpy as jnp
from jax import lax
from jax.sharding import PartitionSpec as P

LON = 4096
NDIR = 36
NFREQ = 36
WSTEPS = 2


two_pi = 2.0 * math.pi
gravity = 9.81
base_freq = 0.04177
courant = 0.45
wind_scale = 10.0
growth = 0.05
dissipation = 0.5
energy_ref = 8.0
mid_freq = 0.2
stress_coef = 0.03
drag_coef = 0.0012
stress_floor = 0.02


def copy_for_each(shard, axis):
    copies = jnp.broadcast_to(shard, (lax.axis_size(axis), *shard.shape))
    return lax.all_to_all(copies, axis, split_axis=0, concat_axis=0, tiled=True)


def laid_out(blocks, dim):
    shape = list(blocks.shape[1:])
    shape[dim] *= blocks.shape[0]
    return jnp.moveaxis(blocks, 0, dim).reshape(shape)


def gathered_copies(shard, axis, dim):
    blocks = copy_for_each(shard, axis)
    return laid_out(blocks, dim)


def extended(shard, sides, width):
    edges = {}
    for axis, dim in sides:
        devices, length = (lax.axis_size(axis), shard.shape[dim])
        up = [(i, (i + 1) % devices) for i in range(devices - 1)]
        last = lax.slice_in_dim(shard, length - width, length, axis=dim)
        initial = lax.slice_in_dim(shard, 0, width, axis=dim)
        edges[dim] = (
            lax.ppermute(last, axis, up),
            lax.ppermute(initial, axis, [(b, a) for a, b in up]),
        )
    done = []
    for _, dim in sides:
        low, high = edges[dim]
        around = [(width, width) if d in done else (0, 0) for d in range(shard.ndim)]
        shard = jnp.concatenate([jnp.pad(low, around), shard, jnp.pad(high, around)], axis=dim)
        done.append(dim)
    return shard


def cycle_tables(cycle_counts, slot_index, wave_count):
    orders = jnp.arange(wave_count, dtype=jnp.int32)
    remain = orders[None, :, None] * slot_index[None, None, :] % cycle_counts[:, None, None]
    phases = two_pi * remain.astype(jnp.float32) / cycle_counts.astype(jnp.float32)[:, None, None]
    weight = jnp.where(orders == 0, 1.0, 2.0).astype(jnp.float32)[None, :, None]
    active = slot_index[None, None, :] < cycle_counts[:, None, None]
    cosine_part = jnp.where(active, weight * jnp.cos(phases), 0.0)
    sine_part = jnp.where(active, -weight * jnp.sin(phases), 0.0)
    return jnp.stack([cosine_part, sine_part], axis=1).astype(jnp.bfloat16)


def bin_constants(directions, freq_index):
    heading = two_pi * (directions.astype(jnp.float32) + 0.5) / NDIR
    freq_step = 35.0 / (NFREQ - 1)
    period_ratio = jnp.exp(-math.log(1.1) * freq_step * freq_index.astype(jnp.float32))
    frequency = base_freq / period_ratio
    cosine_dir = jnp.cos(heading)
    sine_dir = jnp.sin(heading)
    drift_east = courant * period_ratio * cosine_dir
    drift_north = courant * period_ratio * sine_dir
    inverse_speed = two_pi * frequency / gravity
    bin_width = 0.1 * frequency * (two_pi / NDIR)
    return (frequency, cosine_dir, sine_dir, drift_east, drift_north, inverse_speed, bin_width)


def advect(padded, drift_east, drift_north):
    centre = padded[1:-1, 1:-1]
    western = padded[1:-1, :-2]
    eastern = padded[1:-1, 2:]
    southern = padded[:-2, 1:-1]
    northern = padded[2:, 1:-1]
    east_pos = jnp.maximum(drift_east, 0.0)
    east_neg = jnp.minimum(drift_east, 0.0)
    north_pos = jnp.maximum(drift_north, 0.0)
    north_neg = jnp.minimum(drift_north, 0.0)
    return (
        centre
        - east_pos * (centre - western)
        - east_neg * (eastern - centre)
        - north_pos * (centre - southern)
        - north_neg * (northern - centre)
    )


def wind_terms(density, east_wind, north_wind, cosine_dir, sine_dir, inverse_speed, bin_width):
    alignment = (
        east_wind[..., None] * cosine_dir + north_wind[..., None] * sine_dir
    ) * inverse_speed
    wind_gain = growth * jnp.maximum(alignment - 1.0, 0.0)
    energy_part = jnp.sum(density * bin_width, axis=-1)
    stress_part = jnp.sum(wind_gain * density * alignment * bin_width, axis=-1)
    return (wind_gain, energy_part, stress_part)


def finish(density, wind_gain, energy, stress, east_wind, north_wind, frequency):
    decay_rate = dissipation * (frequency / mid_freq) * jnp.square(energy / energy_ref)[..., None]
    spectra_after = density * (1.0 + wind_gain) / (1.0 + decay_rate)
    air_stress = drag_coef * (east_wind * east_wind + north_wind * north_wind) + stress_floor
    roughness = jnp.sqrt(1.0 + stress_coef * stress / air_stress)
    return (spectra_after, roughness)


def per_device(
    legendre, coefficients, cycle_points, spectra, sea_mask, wind_column, roughness_source
):
    band_index = lax.axis_index("aa")
    column_index = lax.axis_index("ba")
    half_index = lax.axis_index("comp")
    wave_block = legendre.shape[0]
    degrees = jnp.arange(legendre.shape[2], dtype=jnp.int32)
    orders_local = band_index * wave_block + jnp.arange(wave_block, dtype=jnp.int32)
    masked = jnp.where(
        degrees[None, None, :] >= orders_local[:, None, None], legendre, jnp.zeros((), jnp.bfloat16)
    )
    partial_fourier = jnp.einsum(
        "mln,smpcn->smlpc", masked, coefficients, preferred_element_type=jnp.float32
    ).astype(jnp.bfloat16)
    cycle_fourier = lax.all_to_all(partial_fourier, "aa", split_axis=2, concat_axis=1, tiled=True)
    wave_count = cycle_fourier.shape[1]
    cycles_local = cycle_fourier.shape[2]
    slots_local = LON // lax.axis_size("ba")
    counts = lax.dynamic_slice_in_dim(cycle_points, band_index * cycles_local, cycles_local)
    own_slots = column_index * slots_local + jnp.arange(slots_local, dtype=jnp.int32)
    tables = cycle_tables(counts, own_slots, wave_count)
    grid_winds = jnp.einsum(
        "smlpc,lpmx->slcx",
        gathered_copies(cycle_fourier, "ba", 4),
        tables,
        preferred_element_type=jnp.float32,
    ).astype(jnp.bfloat16)
    lowest = grid_winds[:, :, 0, :]
    wind_levels = lax.all_gather(lowest, "comp", axis=0, tiled=True)
    rows_local = spectra.shape[0]
    columns_local = spectra.shape[1]
    cycle_rows = rows_local // cycles_local
    own_columns = lax.dynamic_slice_in_dim(
        wind_column, column_index * columns_local, columns_local, 1
    )
    portion = gathered_copies(wind_levels, "ba", 2)
    repeated = jnp.repeat(portion, cycle_rows, axis=1)
    inside = (own_columns >= 0) & (own_columns < portion.shape[2])
    position = jnp.clip(own_columns, 0, portion.shape[2] - 1)
    picked = jnp.take_along_axis(
        repeated, jnp.broadcast_to(position[None], (2,) + position.shape), axis=2
    )
    wind_pair = jnp.where(inside[None], picked.astype(jnp.float32), 0.0)
    east_wind = wind_scale * wind_pair[0]
    north_wind = wind_scale * wind_pair[1]
    half_bins = spectra.shape[2]
    dir_half = half_bins // NFREQ
    bin_index = jnp.arange(half_bins, dtype=jnp.int32)
    frequency, cosine_dir, sine_dir, drift_east, drift_north, inverse_speed, bin_width = (
        bin_constants(half_index * dir_half + bin_index // NFREQ, bin_index % NFREQ)
    )
    sea_float = sea_mask.astype(jnp.float32)[:, :, None]
    density = spectra * sea_float
    for substep in range(WSTEPS):
        padded = extended(density, (("aa", 0), ("ba", 1)), 1)
        density = advect(padded, drift_east, drift_north) * sea_float
    wind_gain, energy_part, stress_part = wind_terms(
        density, east_wind, north_wind, cosine_dir, sine_dir, inverse_speed, bin_width
    )
    energy, stress = lax.psum((energy_part, stress_part), "comp")
    wave_spectra, roughness = finish(
        density, wind_gain, energy, stress, east_wind, north_wind, frequency
    )
    band_ratio = gathered_copies(roughness, "ba", 1).reshape(-1)
    values = jnp.take(band_ratio, roughness_source)
    slot_index = column_index * slots_local + jnp.arange(slots_local, dtype=jnp.int32)
    active = slot_index[None, :] < counts[:, None]
    charnock = jnp.where(active, values, 0.0)
    return (grid_winds, wave_spectra, charnock)


def solution(mesh):
    in_specs = (
        P("aa", None, None),
        P("comp", "aa", None, "ba", None),
        P(),
        P("aa", "ba", "comp"),
        P("aa", "ba"),
        P("aa", None),
        P("aa", "ba"),
    )
    out_specs = (P("comp", "aa", None, "ba"), P("aa", "ba", "comp"), P("aa", "ba"))
    return jax.shard_map(
        per_device, mesh=mesh, in_specs=in_specs, out_specs=out_specs, check_vma=False
    )
```

profile of v0, /device:TPU:128, one launch (start us, length us, event | category | flops | bytes accessed | tf_op | source)
XLA Modules:
  0.0 175.3 jit_solution(13983427964244145663)
XLA Ops:
  0.8 1.3 copy-done
  2.1 4.7 %fusion.56 = bf16[1,80,32,2,4]{2,4,3,1,0:T(4,128)(2,1)S(1)} fusion(bf16[1,80,2,4,1280]{4,3,2,1,0:T(4,128)(2,1)S(1)} %copy-done, bf16[80,32,1280]{2,1,0:T(8,128)(2,1)} %param.7, pred[80,1280]{1,0:T(8,128)(4,1)S(1)} %iota_compare_fusion), kind=kOutput, calls=%fused_computation.79 | convolution fusion | flops 55726080 | bytes 8335360 | tf_op jit(solution)/shard_map/mln,smpcn->smlpc/dot_general | solution.py:138
  6.8 0.8 copy.12
  7.5 9.8 %all-to-all-start = ((bf16[1,80,32,2,4]{1,4,3,0,2:T(4,128)(2,1)}), bf16[1,80,32,2,4]{1,4,3,0,2:T(4,128)(2,1)S(1)}, u32[]{:S(2)}, u32[]{:S(2)}) async-start(bf16[1,80,32,2,4]{1,4,3,0,2:T(4,128)(2,1)} %copy.12), calls=%async_computation | async-start | bytes 131072 | tf_op jit(solution)/shard_map/all_to_all | solution.py:141
  17.4 1.6 broadcast_multiply_fusion
  19.0 0.7 fusion.95
  19.7 3.4 %collective-permute-start.1 = (f32[1,32,648]{2,1,0:T(8,128)}, f32[1,32,648]{2,1,0:T(8,128)}, u32[]{:S(2)}, u32[]{:S(2)}) collective-permute-start(f32[1,32,648]{2,1,0:T(8,128)} %get-tuple-element.18), channel_id=1, source_target_pairs={{0,16},{16,32},{32,48},{48,64},{64,80},{80,96},{96,112},{1,17},{17... | collective-permute-start | bytes 248840 | tf_op jit(solution)/shard_map/ppermute | solution.py:52
  23.0 8.5 %collective-permute-start.2 = (f32[1,32,648]{2,1,0:T(8,128)S(1)}, f32[1,32,648]{2,1,0:T(8,128)}, u32[]{:S(2)}, u32[]{:S(2)}) collective-permute-start(f32[1,32,648]{2,1,0:T(8,128)S(1)} %get-tuple-element.19), channel_id=1, source_target_pairs={{16,0},{32,16},{48,32},{64,48},{80,64},{96,80},{112,96},{17,1},{33... | collective-permute-start | bytes 248840 | tf_op jit(solution)/shard_map/ppermute | solution.py:53
  31.5 0.7 fusion.94
  32.2 3.5 %collective-permute-start = (f32[16,1,648]{2,1,0:T(1,128)}, f32[16,1,648]{2,1,0:T(1,128)}, u32[]{:S(2)}, u32[]{:S(2)}) collective-permute-start(f32[16,1,648]{2,1,0:T(1,128)} %get-tuple-element.16), channel_id=1, source_target_pairs={{0,1},{1,2},{2,3},{3,4},{4,5},{5,6},{6,7},{7,8},{8,9},{9,10},{10,1... | collective-permute-start | bytes 124424 | tf_op jit(solution)/shard_map/ppermute | solution.py:52
  35.7 1.5 collective-permute-start.3
  37.9 0.9 iota_multiply_fusion
  38.9 1.4 broadcast_compare_fusion
  40.9 36.9 %select_convert_fusion.1 = (bf16[4,1,640,256]{3,2,1,0:T(8,128)(2,1)}, bf16[4,1,640,256]{3,2,1,0:T(8,128)(2,1)}) fusion(f32[640]{0:T(1024)S(1)} %get-tuple-element.25, f32[4]{0:T(128)S(1)} %convert_element_type.108, pred[4]{0:T(512)(128)(4,1)S(1)} %broadcast_compare_fusion.2, s32[4]{0:T(128)S(1)} %get-tuple-element.10, s32[640,256]{1,0:T(8,128)} %iota_multiply_fusion, ...), kind=kLoop, calls=%fused_computation.19 | loop fusion | flops 10485760 | bytes 3282980 | tf_op jit(solution)/shard_map/convert
  77.8 0.6 broadcast_multiply_fusion.3
  78.6 1.0 broadcast_in_dim.128
  79.6 8.2 %all-to-all-start.1 = ((bf16[16,1,640,4,2,4]{2,5,4,3,1,0:T(4,128)(2,1)}), bf16[16,1,640,4,2,4]{2,5,4,3,1,0:T(4,128)(2,1)}, u32[]{:S(2)}, u32[]{:S(2)}) async-start(bf16[16,1,640,4,2,4]{2,5,4,3,1,0:T(4,128)(2,1)} %broadcast_in_dim.128), calls=%async_computation.1 | async-start | bytes 1310720 | tf_op jit(solution)/shard_map/all_to_all | solution.py:30
  88.4 0.6 fusion.86
  89.1 0.6 broadcast_multiply_fusion.2
  89.8 3.1 %fusion.33 = f32[16,32,648]{2,1,0:T(8,128)S(1)} fusion(f32[16,32,648]{2,1,0:T(8,128)S(1)} %broadcast_multiply_fusion, f32[1,32,648]{2,1,0:T(8,128)} %collective-permute-done.2, f32[1,32,648]{2,1,0:T(8,128)} %collective-permute-done.1, f32[16,1,648]{2,1,0:T(1,128)} %collective-permute-done.3, f32[16,1,648]{2,1,0:T(1,128)} %collective-permute-done, ...), kind=kLoop, calls=%fused_computation.50 | loop fusion | flops 8957952 | bytes 2915456 | tf_op jit(solution)/shard_map/mul | solution.py:182
  92.9 1.1 copy-done.1
  94.1 0.7 fusion.93
  94.8 1.9 %collective-permute-start.5 = (f32[1,32,648]{2,1,0:T(8,128)}, f32[1,32,648]{2,1,0:T(8,128)}, u32[]{:S(2)}, u32[]{:S(2)}) collective-permute-start(f32[1,32,648]{2,1,0:T(8,128)} %get-tuple-element.14), channel_id=1, source_target_pairs={{0,16},{16,32},{32,48},{48,64},{64,80},{80,96},{96,112},{1,17},{17... | collective-permute-start | bytes 248840 | tf_op jit(solution)/shard_map/ppermute | solution.py:52
  96.7 10.2 %collective-permute-start.6 = (f32[1,32,648]{2,1,0:T(8,128)}, f32[1,32,648]{2,1,0:T(8,128)}, u32[]{:S(2)}, u32[]{:S(2)}) collective-permute-start(f32[1,32,648]{2,1,0:T(8,128)} %get-tuple-element.15), channel_id=1, source_target_pairs={{16,0},{32,16},{48,32},{64,48},{80,64},{96,80},{112,96},{17,1},{33... | collective-permute-start | bytes 248840 | tf_op jit(solution)/shard_map/ppermute | solution.py:53
  106.9 1.3 copy.15
  108.2 1.0 reshape.263
  109.2 2.6 %fusion.61 = bf16[1,4,64,256]{3,2,1,0:T(8,128)(2,1)S(1)} fusion(bf16[640,4,2,64]{0,3,2,1:T(8,128)(2,1)} %reshape.263, bf16[4,1,640,256]{3,2,1,0:T(8,128)(2,1)} %get-tuple-element.21, bf16[4,1,640,256]{3,2,1,0:T(8,128)(2,1)} %get-tuple-element.20), kind=kOutput, calls=%fused_computation.80 | convolution fusion | flops 173080576 | bytes 3407872 | tf_op jit(solution)/shard_map/smlpc,lpmx->slcx/dot_general | solution.py:148
  111.8 0.6 copy-done.21
  112.4 1.8 %all-gather = bf16[2,4,1,256]{3,1,2,0:T(4,128)(2,1)S(1)} all-gather(bf16[1,4,1,256]{3,1,2,0:T(4,128)(2,1)S(1)} %copy.16), channel_id=2, replica_groups=mesh['comp'=2,'aa'=8,'ba'=16] {'comp'}, dimensions={0}, use_global_device_ids=true | all-gather | bytes 6144 | tf_op jit(solution)/shard_map/all_gather | solution.py:155
  114.2 0.6 broadcast_in_dim.133
  114.8 7.5 %all-to-all-start.2 = ((bf16[16,2,4,256]{3,2,1,0:T(4,128)(2,1)}), bf16[16,2,4,256]{3,2,1,0:T(4,128)(2,1)S(1)}, u32[]{:S(2)}, u32[]{:S(2)}) async-start(bf16[16,2,4,256]{3,2,1,0:T(4,128)(2,1)} %broadcast_in_dim.133), calls=%async_computation.2 | async-start | bytes 131072 | tf_op jit(solution)/shard_map/all_to_all | solution.py:30
  122.3 0.7 fusion.92
  123.0 4.4 %collective-permute-start.4 = (f32[16,1,648]{2,1,0:T(1,128)}, f32[16,1,648]{2,1,0:T(1,128)}, u32[]{:S(2)}, u32[]{:S(2)}) collective-permute-start(f32[16,1,648]{2,1,0:T(1,128)} %get-tuple-element.12), channel_id=1, source_target_pairs={{0,1},{1,2},{2,3},{3,4},{4,5},{5,6},{6,7},{7,8},{8,9},{9,10},{10,1... | collective-permute-start | bytes 124424 | tf_op jit(solution)/shard_map/ppermute | solution.py:52
  127.4 1.3 collective-permute-start.7
  128.7 1.7 all-to-all-done.2
  130.5 0.8 broadcast_in_dim.134
  131.3 1.0 reshape.265
  132.3 10.6 %gather_fusion.1 = bf16[1024]{0:T(1024)(128)(2,1)S(1)} fusion(bf16[2,16,4096]{2,1,0:T(8,128)(2,1)S(1)} %reshape.265, s32[1024]{0:T(1024)S(1)} %reshape.274), kind=kCustom, calls=%fused_computation.1 | custom fusion | bytes 16384 | tf_op jit(solution)/shard_map/jit(take_along_axis)/gather | solution.py:166
  143.0 0.7 convert_select_fusion
  143.8 4.8 %multiply_reduce_fusion = (f32[16,32]{1,0:T(8,128)S(1)}, f32[16,32]{1,0:T(8,128)S(1)}, f32[16,32,648]{2,1,0:T(8,128)}) fusion(f32[648]{0:T(1024)} %broadcast_multiply_fusion.1, f32[648]{0:T(1024)} %broadcast_multiply_fusion.3, f32[648]{0:T(1024)} %get-tuple-element.31, f32[16,32]{1,0:T(8,128)S(1)} %get-tuple-element.24, f32[648]{0:T(1024)} %get-tuple-element.32, ...), kind=kLoop, calls=%fused_computation.71 | loop fusion | flops 13270016 | bytes 2934016 | tf_op jit(solution)/shard_map/reduce_sum | solution.py:114
  148.6 3.3 %all-reduce.4 = (f32[16,32]{1,0:T(8,128)S(1)}, f32[16,32]{1,0:T(8,128)S(1)}) all-reduce(f32[16,32]{1,0:T(8,128)S(1)} %get-tuple-element.4, f32[16,32]{1,0:T(8,128)S(1)} %get-tuple-element.3), channel_id=1, replica_groups=mesh['comp'=2,'aa'=8,'ba'=16] {'comp'}, use_global_device_ids=true, to_apply=%region_1.2 | all-reduce | flops 1024 | bytes 8192 | tf_op jit(solution)/shard_map/psum | solution.py:186
  151.9 0.7 reshape.285
  152.6 6.2 %all-to-all-start.3 = ((f32[16,1,512]{2,1,0:T(1,128)}), f32[16,1,512]{2,1,0:T(1,128)S(1)}, u32[]{:S(2)}, u32[]{:S(2)}) async-start(f32[16,1,512]{2,1,0:T(1,128)} %reshape.285), calls=%async_computation.3 | async-start | bytes 65536 | tf_op jit(solution)/shard_map/all_to_all | solution.py:30
  158.9 3.3 %add_divide_fusion = f32[16,32,648]{2,1,0:T(8,128)} fusion(f32[16,32,648]{2,1,0:T(8,128)} %get-tuple-element.7, f32[16,32]{1,0:T(8,128)S(1)} %multiply_multiply_fusion, f32[648]{0:T(1024)S(1)} %copy-done.11, f32[648]{0:T(1024)S(1)} %copy-done.7, f32[648]{0:T(1024)S(1)} %copy-done.8, f32[16,32]{1,0:T(8,128)S(1)} %get-tuple-element.24, f32[648]{0:T(1024)S(1)} %copy-done.9, ...), kind=kLoop, calls=%fused_computation.72 | loop fusion | flops 3981312 | bytes 2670720 | tf_op jit(solution)/shard_map/div | solution.py:120
  162.2 4.7 %all-to-all-done.3 = f32[16,1,512]{2,1,0:T(1,128)S(1)} async-done(((f32[16,1,512]{2,1,0:T(1,128)}), f32[16,1,512]{2,1,0:T(1,128)S(1)}, u32[]{:S(2)}, u32[]{:S(2)}) %all-to-all-start.3) | async-done | bytes 32800 | tf_op jit(solution)/shard_map/all_to_all | solution.py:30
  167.4 0.7 reduce
  168.4 6.2 %gather_fusion = f32[1024]{0:T(1024)S(1)} fusion(f32[8192]{0:T(1024)S(1)} %reshape_reshape.3, s32[1024]{0:T(1024)S(1)} %copy-done.14), kind=kCustom, calls=%fused_computation | custom fusion | bytes 12288 | tf_op jit(solution)/shard_map/jit(_take)/gather | solution.py:191
  174.6 0.7 select_select_fusion
  (85 shorter events, 3.3 us)
Async XLA Ops:
  0.6 1.4 copy-start
  2.1 15.3 %copy-start.17 = (s32[16,32]{1,0:T(8,128)S(1)}, s32[16,32]{1,0:T(8,128)}, u32[]{:S(2)}) copy-start(s32[16,32]{1,0:T(8,128)} %param.11) | copy-start | bytes 6148
  7.5 70.9 %all-to-all-start = ((bf16[1,80,32,2,4]{1,4,3,0,2:T(4,128)(2,1)}), bf16[1,80,32,2,4]{1,4,3,0,2:T(4,128)(2,1)S(1)}, u32[]{:S(2)}, u32[]{:S(2)}) async-start(bf16[1,80,32,2,4]{1,4,3,0,2:T(4,128)(2,1)} %copy.12), calls=%async_computation | async-start | bytes 131072 | tf_op jit(solution)/shard_map/all_to_all | solution.py:141
  17.4 19.8 %copy-start.20 = (s32[32]{0:T(128)S(1)}, s32[32]{0:T(128)}, u32[]{:S(2)}) copy-start(s32[32]{0:T(128)} %param.9) | copy-start | bytes 388
  17.4 22.9 %copy-start.12 = (s32[4,256]{1,0:T(4,128)S(1)}, s32[4,256]{1,0:T(4,128)}, u32[]{:S(2)}) copy-start(s32[4,256]{1,0:T(4,128)} %param.13) | copy-start | bytes 12292
  19.7 70.1 %collective-permute-start.1 = (f32[1,32,648]{2,1,0:T(8,128)}, f32[1,32,648]{2,1,0:T(8,128)}, u32[]{:S(2)}, u32[]{:S(2)}) collective-permute-start(f32[1,32,648]{2,1,0:T(8,128)} %get-tuple-element.18), channel_id=1, source_target_pairs={{0,16},{16,32},{32,48},{48,64},{64,80},{80,96},{96,112},{1,17},{17... | collective-permute-start | bytes 248840 | tf_op jit(solution)/shard_map/ppermute | solution.py:52
  23.0 66.8 %collective-permute-start.2 = (f32[1,32,648]{2,1,0:T(8,128)S(1)}, f32[1,32,648]{2,1,0:T(8,128)}, u32[]{:S(2)}, u32[]{:S(2)}) collective-permute-start(f32[1,32,648]{2,1,0:T(8,128)S(1)} %get-tuple-element.19), channel_id=1, source_target_pairs={{16,0},{32,16},{48,32},{64,48},{80,64},{96,80},{112,96},{17,1},{33... | collective-permute-start | bytes 248840 | tf_op jit(solution)/shard_map/ppermute | solution.py:53
  32.2 57.6 %collective-permute-start = (f32[16,1,648]{2,1,0:T(1,128)}, f32[16,1,648]{2,1,0:T(1,128)}, u32[]{:S(2)}, u32[]{:S(2)}) collective-permute-start(f32[16,1,648]{2,1,0:T(1,128)} %get-tuple-element.16), channel_id=1, source_target_pairs={{0,1},{1,2},{2,3},{3,4},{4,5},{5,6},{6,7},{7,8},{8,9},{9,10},{10,1... | collective-permute-start | bytes 124424 | tf_op jit(solution)/shard_map/ppermute | solution.py:52
  35.7 54.0 %collective-permute-start.3 = (f32[16,1,648]{2,1,0:T(1,128)S(1)}, f32[16,1,648]{2,1,0:T(1,128)}, u32[]{:S(2)}, u32[]{:S(2)}) collective-permute-start(f32[16,1,648]{2,1,0:T(1,128)S(1)} %get-tuple-element.17), channel_id=1, source_target_pairs={{1,0},{2,1},{3,2},{4,3},{5,4},{6,5},{7,6},{8,7},{9,8},{10,9},{11,1... | collective-permute-start | bytes 124424 | tf_op jit(solution)/shard_map/ppermute | solution.py:53
  37.3 0.6 copy-start.18
  37.3 0.5 copy-start.15
  38.8 51.0 %copy-start.3 = (f32[648]{0:T(1024)}, f32[648]{0:T(1024)S(1)}, u32[]{:S(2)}) copy-start(f32[648]{0:T(1024)S(1)} %get-tuple-element.27) | copy-start | bytes 7780
  38.8 51.0 %copy-start.4 = (f32[648]{0:T(1024)}, f32[648]{0:T(1024)S(1)}, u32[]{:S(2)}) copy-start(f32[648]{0:T(1024)S(1)} %get-tuple-element.28) | copy-start | bytes 7780
  38.9 50.9 %copy-start.5 = (f32[648]{0:T(1024)}, f32[648]{0:T(1024)S(1)}, u32[]{:S(2)}) copy-start(f32[648]{0:T(1024)S(1)} %get-tuple-element.29) | copy-start | bytes 7780
  38.9 50.9 %copy-start.6 = (f32[648]{0:T(1024)}, f32[648]{0:T(1024)S(1)}, u32[]{:S(2)}) copy-start(f32[648]{0:T(1024)S(1)} %get-tuple-element.30) | copy-start | bytes 7780
  40.3 48.8 %copy-start.10 = (pred[16,32]{1,0:T(8,128)(4,1)}, pred[16,32]{1,0:T(8,128)(4,1)S(1)}, u32[]{:S(2)}) copy-start(pred[16,32]{1,0:T(8,128)(4,1)S(1)} %get-tuple-element.8) | copy-start | bytes 1540
  79.6 27.2 %all-to-all-start.1 = ((bf16[16,1,640,4,2,4]{2,5,4,3,1,0:T(4,128)(2,1)}), bf16[16,1,640,4,2,4]{2,5,4,3,1,0:T(4,128)(2,1)}, u32[]{:S(2)}, u32[]{:S(2)}) async-start(bf16[16,1,640,4,2,4]{2,5,4,3,1,0:T(4,128)(2,1)} %broadcast_in_dim.128), calls=%async_computation.1 | async-start | bytes 1310720 | tf_op jit(solution)/shard_map/all_to_all | solution.py:30
  92.9 1.1 copy-start.1
  94.8 49.0 %collective-permute-start.5 = (f32[1,32,648]{2,1,0:T(8,128)}, f32[1,32,648]{2,1,0:T(8,128)}, u32[]{:S(2)}, u32[]{:S(2)}) collective-permute-start(f32[1,32,648]{2,1,0:T(8,128)} %get-tuple-element.14), channel_id=1, source_target_pairs={{0,16},{16,32},{32,48},{48,64},{64,80},{80,96},{96,112},{1,17},{17... | collective-permute-start | bytes 248840 | tf_op jit(solution)/shard_map/ppermute | solution.py:52
  96.7 47.0 %collective-permute-start.6 = (f32[1,32,648]{2,1,0:T(8,128)}, f32[1,32,648]{2,1,0:T(8,128)}, u32[]{:S(2)}, u32[]{:S(2)}) collective-permute-start(f32[1,32,648]{2,1,0:T(8,128)} %get-tuple-element.15), channel_id=1, source_target_pairs={{16,0},{32,16},{48,32},{64,48},{80,64},{96,80},{112,96},{17,1},{33... | collective-permute-start | bytes 248840 | tf_op jit(solution)/shard_map/ppermute | solution.py:53
  109.2 13.2 %copy-start.2 = (f32[16,32,648]{2,1,0:T(8,128)S(1)}, f32[16,32,648]{2,1,0:T(8,128)}, u32[]{:S(2)}) copy-start(f32[16,32,648]{2,1,0:T(8,128)} %copy-done.1) | copy-start | bytes 3981316
  111.8 0.7 copy-start.21
  114.8 15.6 %all-to-all-start.2 = ((bf16[16,2,4,256]{3,2,1,0:T(4,128)(2,1)}), bf16[16,2,4,256]{3,2,1,0:T(4,128)(2,1)S(1)}, u32[]{:S(2)}, u32[]{:S(2)}) async-start(bf16[16,2,4,256]{3,2,1,0:T(4,128)(2,1)} %broadcast_in_dim.133), calls=%async_computation.2 | async-start | bytes 131072 | tf_op jit(solution)/shard_map/all_to_all | solution.py:30
  123.0 20.7 %collective-permute-start.4 = (f32[16,1,648]{2,1,0:T(1,128)}, f32[16,1,648]{2,1,0:T(1,128)}, u32[]{:S(2)}, u32[]{:S(2)}) collective-permute-start(f32[16,1,648]{2,1,0:T(1,128)} %get-tuple-element.12), channel_id=1, source_target_pairs={{0,1},{1,2},{2,3},{3,4},{4,5},{5,6},{6,7},{7,8},{8,9},{9,10},{10,1... | collective-permute-start | bytes 124424 | tf_op jit(solution)/shard_map/ppermute | solution.py:52
  127.4 16.3 %collective-permute-start.7 = (f32[16,1,648]{2,1,0:T(1,128)S(1)}, f32[16,1,648]{2,1,0:T(1,128)}, u32[]{:S(2)}, u32[]{:S(2)}) collective-permute-start(f32[16,1,648]{2,1,0:T(1,128)S(1)} %get-tuple-element.13), channel_id=1, source_target_pairs={{1,0},{2,1},{3,2},{4,3},{5,4},{6,5},{7,6},{8,7},{9,8},{10,9},{11,1... | collective-permute-start | bytes 124424 | tf_op jit(solution)/shard_map/ppermute | solution.py:53
  143.7 15.1 %copy-start.7 = (f32[648]{0:T(1024)S(1)}, f32[648]{0:T(1024)}, u32[]{:S(2)}) copy-start(f32[648]{0:T(1024)} %broadcast_multiply_fusion.3) | copy-start | bytes 7780
  143.7 15.1 %copy-start.8 = (f32[648]{0:T(1024)S(1)}, f32[648]{0:T(1024)}, u32[]{:S(2)}) copy-start(f32[648]{0:T(1024)} %get-tuple-element.31) | copy-start | bytes 7780
  143.8 15.1 %copy-start.9 = (f32[648]{0:T(1024)S(1)}, f32[648]{0:T(1024)}, u32[]{:S(2)}) copy-start(f32[648]{0:T(1024)} %get-tuple-element.32) | copy-start | bytes 7780
  143.8 15.1 %copy-start.11 = (f32[648]{0:T(1024)S(1)}, f32[648]{0:T(1024)}, u32[]{:S(2)}) copy-start(f32[648]{0:T(1024)} %broadcast_multiply_fusion.2) | copy-start | bytes 7780
  152.6 14.2 %all-to-all-start.3 = ((f32[16,1,512]{2,1,0:T(1,128)}), f32[16,1,512]{2,1,0:T(1,128)S(1)}, u32[]{:S(2)}, u32[]{:S(2)}) async-start(f32[16,1,512]{2,1,0:T(1,128)} %reshape.285), calls=%async_computation.3 | async-start | bytes 65536 | tf_op jit(solution)/shard_map/all_to_all | solution.py:30
  158.9 9.4 %copy-start.14 = (s32[1024]{0:T(1024)S(1)}, s32[1024]{0:T(1024)}, u32[]{:S(2)}) copy-start(s32[1024]{0:T(1024)} %broadcast_clamp_fusion) | copy-start | bytes 12292
  168.4 6.2 %copy-start.13 = (s32[4,256]{1,0:T(4,128)S(1)}, s32[4,256]{1,0:T(4,128)}, u32[]{:S(2)}) copy-start(s32[4,256]{1,0:T(4,128)} %param.13) | copy-start | bytes 12292
  168.4 6.2 %copy-start.16 = (s32[256]{0:T(256)S(1)}, s32[256]{0:T(256)}, u32[]{:S(2)}) copy-start(s32[256]{0:T(256)} %copy-done.15) | copy-start | bytes 3076
  168.4 6.2 %copy-start.19 = (s32[4]{0:T(128)S(1)}, s32[4]{0:T(128)}, u32[]{:S(2)}) copy-start(s32[4]{0:T(128)} %copy-done.18) | copy-start | bytes 52
where the time goes:
time: 176 us; the launch traced here: 175 us
  starting transfers between devices  66.3 us (38%)
  other arithmetic  57.6 us (33%)
  local copies, waits for them, and re-layouts  31.4 us (18%)
  matrix products  7.26 us (4%)
  waiting for transfers between devices  6.4 us (4%)
  blocking collectives  5.07 us (3%)
    another operation x1, other arithmetic  36.9 us
    all_to_all x3, starting transfers between devices, copy_for_each(): return lax.all_to_all(copies, axis, split_axis=0, concat_axis=0, tiled=True)  21.9 us
    ppermute x4, starting transfers between devices, extended(): lax.ppermute(initial, axis, [(b, a) for a, b in up])  21.4 us
    ppermute x4, starting transfers between devices, extended(): lax.ppermute(last, axis, up)  13.2 us
    gather x3, local copies, waits for them, and re-layouts, per_device(): jnp.take_along_axis(repeated, jnp.broadcast_to(position[None], (2,) + pos...  10.8 us
    all_to_all x1, starting transfers between devices, per_device(): lax.all_to_all(partial_fourier, 'aa', split_axis=2, concat_axis=1, tiled=...  9.84 us
    all_to_all x3, waiting for transfers between devices, copy_for_each(): return lax.all_to_all(copies, axis, split_axis=0, concat_axis=0, tiled=True)  6.38 us
    gather x2, local copies, waits for them, and re-layouts, per_device(): values = jnp.take(band_ratio, roughness_source)  6.16 us
  transfers between devices with their start and end apart: 12, of which 2 were waited for; matrix products, arithmetic and copies ran while one was open for 42% of the time, Pallas kernels for 0%

commit v1 on v0

v1 whole, which is shorter than its diff:
```python
import functools
import math

import numpy as np

import jax
import jax.numpy as jnp
from jax import lax
from jax.experimental import pallas as pl
from jax.experimental.pallas import tpu as pltpu
from jax.sharding import PartitionSpec as P

LON = 4096
NDIR = 36
NFREQ = 36
F32 = jnp.float32
BF16 = jnp.bfloat16
MESH = pl.DeviceIdType.MESH

N_A = 8
N_B = 16
N_X = 4
N_Z = 4
WAVES = 640
BLOCK = WAVES // N_A
CYCLES = 4
SLOTS = LON // N_B
ROWS = 16
COLS = 32
HALF = NDIR * NFREQ // 2
POINTS = 128
TILES = [(j, min(128, HALF - j)) for j in range(0, HALF, 128)]


def bin_table():
    b = np.arange(NDIR * NFREQ)
    theta = 2 * np.pi * (b // NFREQ + 0.5) / NDIR
    ratio = np.exp(-math.log(1.1) * (b % NFREQ))
    freq = 0.04177 / ratio
    east = 0.45 * ratio * np.cos(theta)
    north = 0.45 * ratio * np.sin(theta)
    q = 2 * np.pi * freq / 9.81
    width = 0.1 * freq * (2 * np.pi / NDIR)
    rows = [
        np.abs(east),
        np.abs(north),
        1.0 - np.abs(east) - np.abs(north),
        np.sign(east),
        np.sign(north),
        10.0 * q * np.cos(theta),
        10.0 * q * np.sin(theta),
        width,
        0.5 * freq / 0.2,
    ]
    rows += [np.zeros_like(freq)] * (16 - len(rows))
    table = np.stack(rows).astype(np.float32)
    return np.stack([table[:, :HALF], table[:, HALF:]])


AE, AN, CC, SE, SN, QE, QN, WB, DF = range(9)


def poly(y2, coefs):
    acc = jnp.full_like(y2, coefs[-1])
    for c in coefs[-2::-1]:
        acc = acc * y2 + c
    return acc


SIN_C = [(-1.0) ** i / math.factorial(2 * i + 1) for i in range(7)]
COS_C = [(-1.0) ** i / math.factorial(2 * i) for i in range(7)]


def turn(mk, count, inv):
    rest = mk - jnp.floor(mk * inv + 0.5) * count
    y = (rest * inv) * math.pi
    y2 = y * y
    s = y * poly(y2, SIN_C)
    c = poly(y2, COS_C)
    return 1.0 - 2.0 * s * s, 2.0 * s * c


def rcopy(src, dst, send, recv, device):
    return pltpu.make_async_remote_copy(
        src_ref=src, dst_ref=dst, send_sem=send, recv_sem=recv, device_id=device, device_id_type=MESH
    )


def diagonal():
    return lax.broadcasted_iota(jnp.int32, (POINTS, 128), 0) == lax.broadcasted_iota(
        jnp.int32, (POINTS, 128), 1
    )


def spread(row):
    kept = jnp.where(diagonal(), jnp.broadcast_to(row, (POINTS, 128)), 0.0)
    return jnp.broadcast_to(jnp.sum(kept, axis=1, keepdims=True), (POINTS, 128))


def kernel(
    cp_ref, msg_ref, spec_ref, pts_ref, rs_ref, cst_ref,
    gw_ref, ws_ref, ch_ref,
    a2a, gath, gperm, l0, table, ca, sa, buf_a, buf_b, d2, edge, edge_in,
    mask_b, east_b, north_b, en, en_in, stress_b, wind, wind_in, st, st_in, rough,
    a_send, a_recv, g_send, g_recv, l_send, l_recv, h_send, h_recv, c_send, c_recv, r_send, r_recv,
):
    s = lax.axis_index("comp")
    a = lax.axis_index("aa")
    b = lax.axis_index("ba")
    x, z = b // N_Z, b % N_Z
    partner = {"comp": 1 - s}

    barrier = pltpu.get_barrier_semaphore()
    pl.semaphore_signal(barrier, inc=1, device_id=partner, device_id_type=MESH)
    for d in range(1, N_A):
        pl.semaphore_signal(barrier, inc=1, device_id={"aa": lax.rem(a + d, N_A)}, device_id_type=MESH)
    for d in range(1, N_B):
        pl.semaphore_signal(barrier, inc=1, device_id={"ba": lax.rem(b + d, N_B)}, device_id_type=MESH)

    for l in range(CYCLES):
        mask_b[pl.ds(l * POINTS, POINTS), :] = spread(pts_ref[l : l + 1, :].astype(F32))

    def first(r, carry):
        m = mask_b[pl.ds(r * COLS, COLS), :]
        for j, w in TILES:
            v = spec_ref[r, :, j : j + w] * m[:, :w]
            buf_a[r + 1, 8 : 8 + COLS, j : j + w] = v
            edge[0, 0, r, :, j : j + w] = v[0:1, :]
            edge[0, 1, r, :, j : j + w] = v[COLS - 1 : COLS, :]
        return carry

    lax.fori_loop(0, ROWS, first, 0)

    pl.semaphore_wait(barrier, N_A + N_B - 1)

    sent = []
    for d in range(1, N_A):
        t = lax.rem(a + d, N_A)
        c = rcopy(msg_ref.at[t], a2a.at[a], a_send.at[d - 1], a_recv.at[a], {"aa": t})
        c.start()
        sent.append(c)

    def halo(buf, step):
        copies = [
            (a < N_A - 1, a > 0, rcopy(
                buf.at[ROWS, pl.ds(8, COLS)], buf.at[0, pl.ds(8, COLS)],
                h_send.at[step, 0], h_recv.at[step, 0], {"aa": lax.rem(a + 1, N_A)})),
            (a > 0, a < N_A - 1, rcopy(
                buf.at[1, pl.ds(8, COLS)], buf.at[ROWS + 1, pl.ds(8, COLS)],
                h_send.at[step, 1], h_recv.at[step, 1], {"aa": lax.rem(a + N_A - 1, N_A)})),
            (b < N_B - 1, b > 0, rcopy(
                edge.at[step, 1], edge_in.at[step, 0],
                h_send.at[step, 2], h_recv.at[step, 2], {"ba": lax.rem(b + 1, N_B)})),
            (b > 0, b < N_B - 1, rcopy(
                edge.at[step, 0], edge_in.at[step, 1],
                h_send.at[step, 3], h_recv.at[step, 3], {"ba": lax.rem(b + N_B - 1, N_B)})),
        ]
        return copies

    def halo_start(copies):
        for can, _, c in copies:
            pl.when(can)(c.start)

    def halo_land(copies, buf, step):
        for i, (_, comes, c) in enumerate(copies):
            pl.when(comes)(c.wait_recv)

            @pl.when(jnp.logical_not(comes))
            def _():
                if i < 2:
                    buf[0 if i == 0 else ROWS + 1, 8 : 8 + COLS, :] = jnp.zeros((COLS, HALF), F32)
                else:
                    edge_in[step, i - 2] = jnp.zeros((ROWS, 1, HALF), F32)

        def place(r, carry):
            for j, w in TILES:
                buf[r + 1, 7:8, j : j + w] = edge_in[step, 0, r, :, j : j + w]
                buf[r + 1, 8 + COLS : 9 + COLS, j : j + w] = edge_in[step, 1, r, :, j : j + w]
            return carry

        lax.fori_loop(0, ROWS, place, 0)

    def halo_sent(copies):
        for can, _, c in copies:
            pl.when(can)(c.wait_send)

    halo_a = halo(buf_a, 0)
    halo_start(halo_a)
    a2a[a] = msg_ref[a]

    def tables(l, k, active, lane, w):
        count = jnp.full((1, w), cp_ref[a * CYCLES + l], jnp.int32).astype(F32)
        inv = 1.0 / count
        u = lax.broadcasted_iota(jnp.int32, (WAVES // 8, w), 0).astype(F32) * 8.0
        cu, su = turn(u * k, count, inv)
        ca[:, :w] = cu
        sa[:, :w] = su
        v = lax.broadcasted_iota(jnp.int32, (8, w), 0).astype(F32)
        cv, sv = turn(v * k, count, inv)
        cv, sv = cv * active, sv * active

        def block(i, carry):
            near = pl.ds(pl.multiple_of(i * 8, 8), 8)
            c8, s8 = ca[near, :w], sa[near, :w]
            for h in range(4):
                j = i * 4 + h
                cs, ss = [], []
                for o in range(2):
                    c0 = c8[h * 2 + o : h * 2 + o + 1, :]
                    s0 = s8[h * 2 + o : h * 2 + o + 1, :]
                    cs.append(c0 * cv - s0 * sv)
                    ss.append(-(s0 * cv) - c0 * sv)
                at = pl.multiple_of(j * 16, 16)
                table[l, pl.ds(at, 16), lane : lane + w] = jnp.concatenate(cs, axis=0).astype(BF16)
                table[l, pl.ds(WAVES + at, 16), lane : lane + w] = jnp.concatenate(ss, axis=0).astype(BF16)
            return carry

        lax.fori_loop(0, WAVES // 64, block, 0)
        top = table[l, 0:16, lane : lane + w].astype(F32)
        row = lax.broadcasted_iota(jnp.int32, (16, w), 0)
        table[l, 0:16, lane : lane + w] = jnp.where(row == 0, top * 0.5, top).astype(BF16)

    slots = lax.broadcasted_iota(jnp.int32, (1, SLOTS), 1) + b * SLOTS
    for l in range(CYCLES):
        active = jnp.where(slots < cp_ref[a * CYCLES + l], 2.0, 0.0)
        tables(l, slots.astype(F32), active, 0, SLOTS)
        tables(l, pts_ref[4 + l : 5 + l, :].astype(F32), 2.0, SLOTS, POINTS)

    for d in range(1, N_A):
        o = lax.rem(a + N_A - d, N_A)
        rcopy(msg_ref.at[0], a2a.at[o], a_send.at[d - 1], a_recv.at[o], {"aa": o}).wait_recv()
    lane = lax.broadcasted_iota(jnp.int32, (16, 128), 1)
    for p in range(2):
        tiles = [jnp.zeros((16, 128), F32) for _ in range(WAVES // 128)]
        for o in range(N_A):
            t, shift = divmod(o * BLOCK, 128)
            piece = a2a[o, :, p * 128 : p * 128 + 128].astype(F32)
            if shift:
                piece = pltpu.roll(piece, shift, axis=1)
                tiles[t] = tiles[t] + jnp.where(lane >= shift, piece, 0.0)
                if shift + BLOCK > 128:
                    tiles[t + 1] = tiles[t + 1] + jnp.where(lane < shift, piece, 0.0)
            else:
                tiles[t] = tiles[t] + piece
        for t, tile in enumerate(tiles):
            gath[b, :, p * WAVES + t * 128 : p * WAVES + t * 128 + 128] = tile.astype(BF16)

            @pl.when(b == 0)
            def _():
                for l in range(CYCLES):
                    l0[p * 4 + l : p * 4 + l + 1, t * 128 : t * 128 + 128] = tile[4 * l : 4 * l + 1, :]

    low = [
        rcopy(l0, l0, l_send.at[d - 1], l_recv.at[0], {"ba": lax.rem(b + d, N_B)}) for d in range(1, N_B)
    ]

    @pl.when(b == 0)
    def _():
        for c in low:
            c.start()

    gathers = []

    def give(o, device):
        c = rcopy(gath.at[o], gath.at[o], g_send.at[len(gathers)], g_recv.at[o], {"ba": device})
        c.start()
        gathers.append(c)

    def arrived(o):
        rcopy(gath.at[o], gath.at[o], g_send.at[0], g_recv.at[o], {"ba": o}).wait_recv()

    x_peers = [lax.rem(x + d, N_X) * N_Z + z for d in (1, 3, 2)]
    for d in range(1, N_Z):
        give(b, x * N_Z + lax.rem(z + d, N_Z))
    for t in x_peers:
        give(b, t)

    def upwind(buf, r, j, w):
        c = lambda i: cst_ref[s, i : i + 1, j : j + w]
        here = buf[r + 1, 8 : 8 + COLS, j : j + w]
        ux = jnp.where(c(SE) > 0.0, buf[r + 1, 7 : 7 + COLS, j : j + w], buf[r + 1, 9 : 9 + COLS, j : j + w])
        uy = jnp.where(c(SN) > 0.0, buf[r, 8 : 8 + COLS, j : j + w], buf[r + 2, 8 : 8 + COLS, j : j + w])
        return here * c(CC) + ux * c(AE) + uy * c(AN)

    halo_land(halo_a, buf_a, 0)

    def second(r, carry):
        m = mask_b[pl.ds(r * COLS, COLS), :]
        for j, w in TILES:
            v = upwind(buf_a, r, j, w) * m[:, :w]
            buf_b[r + 1, 8 : 8 + COLS, j : j + w] = v
            edge[1, 0, r, :, j : j + w] = v[0:1, :]
            edge[1, 1, r, :, j : j + w] = v[COLS - 1 : COLS, :]
        return carry

    lax.fori_loop(0, ROWS, second, 0)
    halo_b = halo(buf_b, 1)
    halo_start(halo_b)

    for d in range(1, N_Z):
        o = x * N_Z + lax.rem(z + N_Z - d, N_Z)
        arrived(o)
        for t in x_peers:
            give(o, t)

    @pl.when(b > 0)
    def _():
        low[0].wait_recv()

    lowest = l0[...].astype(BF16)
    for l in range(CYCLES):
        pc = jnp.dot(lowest, table[l, 0:WAVES, SLOTS:], preferred_element_type=F32)
        ps = jnp.dot(lowest, table[l, WAVES:, SLOTS:], preferred_element_type=F32)
        value = (pc[l : l + 1, :] + ps[4 + l : 5 + l, :]).astype(BF16).astype(F32)
        wind[l : l + 1, :] = value
        wind[4 + l : 5 + l, :] = value
    wind_copy = rcopy(wind, wind_in, c_send.at[0], c_recv.at[0], partner)
    wind_copy.start()

    halo_land(halo_b, buf_b, 1)

    def third(r, carry):
        m = mask_b[pl.ds(r * COLS, COLS), :]
        total = jnp.zeros((COLS, 128), F32)
        for j, w in TILES:
            v = upwind(buf_b, r, j, w) * m[:, :w]
            d2[r, :, j : j + w] = v
            part = v * cst_ref[s, WB : WB + 1, j : j + w]
            if w == 128:
                total = total + part
            else:
                rest = jnp.sum(part, axis=1, keepdims=True)
        total = jnp.sum(total, axis=1, keepdims=True) + rest
        en[pl.ds(r * COLS, COLS), :] = jnp.broadcast_to(total, (COLS, 128))
        return carry

    lax.fori_loop(0, ROWS, third, 0)
    energy_copy = rcopy(en, en_in, c_send.at[1], c_recv.at[1], partner)
    energy_copy.start()

    wind_copy.wait_recv()
    mine, other = wind[...], wind_in[...]
    east = jnp.where(s == 0, mine, other)
    north = jnp.where(s == 0, other, mine)
    for l in range(CYCLES):
        east_b[pl.ds(l * POINTS, POINTS), :] = spread(east[l : l + 1, :])
        north_b[pl.ds(l * POINTS, POINTS), :] = spread(north[l : l + 1, :])
    air = 0.0012 * (100.0 * (east * east + north * north)) + 0.02

    def gain_of(e, n, r, j, w):
        c = lambda i: cst_ref[s, i : i + 1, j : j + w]
        align = e[:, :w] * c(QE) + n[:, :w] * c(QN)
        grown = 0.05 * jnp.maximum(align - 1.0, 0.0) * d2[r, :, j : j + w]
        return align, grown

    def fourth(r, carry):
        e = east_b[pl.ds(r * COLS, COLS), :]
        n = north_b[pl.ds(r * COLS, COLS), :]
        total = jnp.zeros((COLS, 128), F32)
        for j, w in TILES:
            align, grown = gain_of(e, n, r, j, w)
            part = grown * align * cst_ref[s, WB : WB + 1, j : j + w]
            if w == 128:
                total = total + part
            else:
                rest = jnp.sum(part, axis=1, keepdims=True)
        total = jnp.sum(total, axis=1, keepdims=True) + rest
        stress_b[pl.ds(r * COLS, COLS), :] = jnp.broadcast_to(total, (COLS, 128))
        return carry

    lax.fori_loop(0, ROWS, fourth, 0)
    for l in range(CYCLES):
        block = stress_b[pl.ds(l * POINTS, POINTS), :]
        row = jnp.sum(jnp.where(diagonal(), block, 0.0), axis=0, keepdims=True)
        st[l : l + 1, :] = row
        st[4 + l : 5 + l, :] = row
    stress_copy = rcopy(st, st_in, c_send.at[2], c_recv.at[2], partner)
    stress_copy.start()

    energy_copy.wait_recv()

    def fifth(r, carry):
        at = pl.ds(r * COLS, COLS)
        e, n = east_b[at, :], north_b[at, :]
        level = (en[at, :] + en_in[at, :]) * 0.125
        square = level * level
        for j, w in TILES:
            _, grown = gain_of(e, n, r, j, w)
            decay = square[:, :w] * cst_ref[s, DF : DF + 1, j : j + w]
            ws_ref[r, :, j : j + w] = (d2[r, :, j : j + w] + grown) / (1.0 + decay)
        return carry

    def roughness():
        stress_copy.wait_recv()
        rough[b] = jnp.sqrt(1.0 + 0.03 * (st[...] + st_in[...]) / air)
        copies = []
        for d in range(1, N_B):
            t = lax.rem(b + d, N_B)
            c = rcopy(rough.at[b], rough.at[b], r_send.at[d - 1], r_recv.at[b], {"ba": t})
            c.start()
            copies.append(c)
        return copies

    lax.fori_loop(0, ROWS, fifth, 0)
    rough_copies = roughness()

    for xd in range(1, N_X):
        for zd in range(N_Z):
            arrived(lax.rem(x + N_X - xd, N_X) * N_Z + lax.rem(z + zd, N_Z))
    out_row = lax.broadcasted_iota(jnp.int32, (256, 256), 0)
    in_row = (out_row % 64 // 4) * 16 + out_row // 64 * 4 + out_row % 4
    order = (lax.broadcasted_iota(jnp.int32, (256, 256), 1) == in_row).astype(F32).astype(BF16)
    for k in range(0, 2 * WAVES, 256):
        part = gath[:, :, k : k + 256].reshape(256, 256)
        gperm[:, k : k + 256] = jnp.dot(order, part, preferred_element_type=F32).astype(BF16)
    for l in range(CYCLES):
        gw_ref[0, l] = jnp.dot(
            gperm[l * 64 : l * 64 + 64, :], table[l, :, 0:SLOTS], preferred_element_type=F32
        ).astype(BF16)

    for d in range(1, N_B):
        o = lax.rem(b + N_B - d, N_B)
        rcopy(rough.at[o], rough.at[o], r_send.at[0], r_recv.at[o], {"ba": o}).wait_recv()
    for l in range(CYCLES):
        source = rs_ref[l : l + 1, :]
        low_part = ((source >> 9) & 3) * 32 + (source & 31)
        high_part = (source >> 5) & 15
        pick = (lax.broadcasted_iota(jnp.int32, (128, SLOTS), 0) == low_part).astype(F32).astype(BF16)
        values = rough[:, l, :]
        h0 = values.astype(BF16)
        r1 = values - h0.astype(F32)
        h1 = r1.astype(BF16)
        h2 = (r1 - h1.astype(F32)).astype(BF16)
        got = [jnp.dot(h, pick, preferred_element_type=F32) for h in (h0, h1, h2)]
        got = got[0] + (got[1] + got[2])
        keep = lax.broadcasted_iota(jnp.int32, (N_B, SLOTS), 0) == high_part
        row = jnp.sum(jnp.where(keep, got, 0.0), axis=0, keepdims=True)
        ch_ref[l : l + 1, :] = jnp.where(slots < cp_ref[a * CYCLES + l], row, 0.0)

    for c in sent + gathers + rough_copies + [wind_copy, energy_copy, stress_copy]:
        c.wait_send()
    halo_sent(halo_a)
    halo_sent(halo_b)

    @pl.when(b == 0)
    def _():
        for c in low:
            c.wait_send()


def per_device(legendre, coefficients, cycle_points, spectra, sea_mask, wind_column, roughness_source):
    band = lax.axis_index("aa")
    column = lax.axis_index("ba")
    degrees = jnp.arange(legendre.shape[2], dtype=jnp.int32)
    orders = band * BLOCK + jnp.arange(BLOCK, dtype=jnp.int32)
    masked = jnp.where(
        degrees[None, None, :] >= orders[:, None, None], legendre, jnp.zeros((), BF16)
    )
    fourier = jnp.einsum(
        "mln,mpcn->mlpc", masked, coefficients[0], preferred_element_type=F32
    ).astype(BF16)
    message = jnp.transpose(fourier.reshape(BLOCK, N_A, CYCLES, 2, 4), (1, 2, 4, 3, 0))
    message = jnp.pad(message, ((0, 0),) * 4 + ((0, 128 - BLOCK),)).reshape(N_A, 16, 256)
    own = lax.dynamic_slice_in_dim(wind_column, column * COLS, COLS, 1)
    points = jnp.concatenate([sea_mask.reshape(4, POINTS), own.reshape(4, POINTS)], axis=0)

    vmem = pl.BlockSpec(memory_space=pltpu.VMEM)
    dma = pltpu.SemaphoreType.DMA
    return pl.pallas_call(
        kernel,
        out_shape=(
            jax.ShapeDtypeStruct((1, CYCLES, 64, SLOTS), BF16),
            jax.ShapeDtypeStruct((ROWS, COLS, HALF), F32),
            jax.ShapeDtypeStruct((CYCLES, SLOTS), F32),
        ),
        in_specs=[pl.BlockSpec(memory_space=pltpu.SMEM)] + [vmem] * 5,
        out_specs=(vmem, vmem, vmem),
        scratch_shapes=[
            pltpu.VMEM((N_A, 16, 256), BF16),
            pltpu.VMEM((N_B, 16, 2 * WAVES), BF16),
            pltpu.VMEM((256, 2 * WAVES), BF16),
            pltpu.VMEM((8, WAVES), F32),
            pltpu.VMEM((CYCLES, 2 * WAVES, SLOTS + POINTS), BF16),
            pltpu.VMEM((WAVES // 8, SLOTS), F32),
            pltpu.VMEM((WAVES // 8, SLOTS), F32),
            pltpu.VMEM((ROWS + 2, COLS + 16, HALF), F32),
            pltpu.VMEM((ROWS + 2, COLS + 16, HALF), F32),
            pltpu.VMEM((ROWS, COLS, HALF), F32),
            pltpu.VMEM((2, 2, ROWS, 1, HALF), F32),
            pltpu.VMEM((2, 2, ROWS, 1, HALF), F32),
            pltpu.VMEM((ROWS * COLS, 128), F32),
            pltpu.VMEM((ROWS * COLS, 128), F32),
            pltpu.VMEM((ROWS * COLS, 128), F32),
            pltpu.VMEM((ROWS * COLS, 128), F32),
            pltpu.VMEM((ROWS * COLS, 128), F32),
            pltpu.VMEM((ROWS * COLS, 128), F32),
            pltpu.VMEM((8, 128), F32),
            pltpu.VMEM((8, 128), F32),
            pltpu.VMEM((8, 128), F32),
            pltpu.VMEM((8, 128), F32),
            pltpu.VMEM((N_B, 8, 128), F32),
            dma((N_A - 1,)), dma((N_A,)),
            dma((N_B - 1,)), dma((N_B,)),
            dma((N_B - 1,)), dma((1,)),
            dma((2, 4)), dma((2, 4)),
            dma((3,)), dma((3,)),
            dma((N_B - 1,)), dma((N_B,)),
        ],
        compiler_params=pltpu.CompilerParams(
            collective_id=0, has_side_effects=True, vmem_limit_bytes=48 * 1024 * 1024
        ),
    )(cycle_points, message, spectra, points, roughness_source, jnp.asarray(bin_table()))


def solution(mesh):
    in_specs = (
        P("aa", None, None),
        P("comp", "aa", None, "ba", None),
        P(),
        P("aa", "ba", "comp"),
        P("aa", "ba"),
        P("aa", None),
        P("aa", "ba"),
    )
    out_specs = (P("comp", "aa", None, "ba"), P("aa", "ba", "comp"), P("aa", "ba"))
    return jax.shard_map(
        per_device, mesh=mesh, in_specs=in_specs, out_specs=out_specs, check_vma=False
    )
```

time: 176 us -> 52.1 us (0.30)
  the two profiles are of different devices: /device:TPU:128 before, /device:TPU:1 now
where the time goes in v1:
time: 52.1 us; the launch traced here: 51.3 us
  Pallas kernels  41.1 us (79%)
  matrix products  4.79 us (9%)
  local copies, waits for them, and re-layouts  4.52 us (9%)
  between operations  0.77 us (1%)
    pallas_call x1, Pallas kernels, per_device(): pl.pallas_call(kernel, out_shape=(jax.ShapeDtypeStruct((1, CYCLES, 64, SL...  41.1 us
    dot_general x1, matrix products, per_device(): jnp.einsum('mln,mpcn->mlpc', masked, coefficients[0], preferred_element_t...  4.79 us
    unnamed x14, local copies, waits for them, and re-layouts  2.5 us

profile of v1, /device:TPU:1, one launch (start us, length us, event | category | flops | bytes accessed | tf_op | source)
XLA Modules:
  0.0 51.3 jit_solution(9851839750401599408)
XLA Ops:
  0.6 0.0 copy-start
  0.7 0.9 %reshape.46 = s32[4,128]{1,0:T(4,128)S(1)} reshape(s32[16,32]{1,0:T(8,128)} %param.12) | data formatting | bytes 4096 | tf_op jit(solution)/shard_map/reshape | solution.py:465
  1.6 0.8 %constant_dynamic-slice_fusion = s32[16,32]{1,0:T(8,128)S(1)} fusion(s32[16,512]{1,0:T(8,128)} %param.13, s32[]{:T(128)S(6)} %select_n.8), kind=kLoop, calls=%fused_computation.10 | loop fusion | bytes 4100 | tf_op jit(solution)/shard_map/dynamic_slice | solution.py:464
  2.3 0.1 reshape.47
  2.4 0.1 iota_compare_fusion
  2.6 0.0 copy-done
  2.6 0.0 copy-start.1
  2.6 0.0 copy-start.2
  2.6 0.0 copy-start.3
  2.6 0.0 copy-start.4
  2.6 4.8 %fusion.6 = bf16[80,32,2,4]{1,3,2,0:T(4,128)(2,1)S(1)} fusion(bf16[1,80,2,4,1280]{4,3,2,1,0:T(4,128)(2,1)S(1)} %copy-done, bf16[80,32,1280]{2,1,0:T(8,128)(2,1)} %param.8, pred[80,1280]{1,0:T(8,128)(4,1)S(1)} %iota_compare_fusion), kind=kOutput, calls=%fused_computation.6 | convolution fusion | flops 55726080 | bytes 8335360 | tf_op jit(solution)/shard_map/mln,mpcn->mlpc/dot_general | solution.py:459
  7.4 0.2 copy.12
  7.6 0.1 copy.15
  7.6 0.1 pad.4.clone
  7.8 0.0 copy-done.1
  7.8 0.0 copy-done.2
  7.8 0.0 copy-done.3
  7.8 0.0 copy-done.4
  7.8 41.1 %shard_map.103 = (bf16[1,4,64,256]{3,2,1,0:T(8,128)(2,1)S(1)}, f32[16,32,648]{2,1,0:T(8,128)S(1)}, f32[4,256]{1,0:T(4,128)S(1)}) custom-call(s32[32]{0:T(128)S(1)} %copy-done.4, bf16[8,16,256]{2,1,0:T(8,128)(2,1)S(1)} %reshape.45.msg_ref, f32[16,32,648]{2,1,0:T(8,128)S(1)} %copy-done.1, s32[8,128]{1,0:T(8,128)S(1)} %pad_add_fusion.pts_ref, ...), custom_call_target="tpu_custom_call" | custom-call | tf_op jit(solution)/shard_map/pallas_call | solution.py:469
  48.9 0.7 %copy.19 = bf16[1,4,64,256]{3,2,1,0:T(8,128)(2,1)} copy(bf16[1,4,64,256]{3,2,1,0:T(8,128)(2,1)S(1)} %get-tuple-element.6) | data formatting | bytes 262144
  49.6 1.1 %copy.20 = f32[16,32,648]{2,1,0:T(8,128)} copy(f32[16,32,648]{2,1,0:T(8,128)S(1)} %get-tuple-element.7) | data formatting | bytes 2654208
  50.7 0.6 %copy.21 = f32[4,256]{1,0:T(4,128)} copy(f32[4,256]{1,0:T(4,128)S(1)} %get-tuple-element.8) | data formatting | bytes 8192
  (3 shorter events, 0.1 us)
Async XLA Ops:
  0.6 1.9 %copy-start = (bf16[1,80,2,4,1280]{4,3,2,1,0:T(4,128)(2,1)S(1)}, bf16[1,80,2,4,1280]{4,3,2,1,0:T(4,128)(2,1)}, u32[]{:S(2)}) copy-start(bf16[1,80,2,4,1280]{4,3,2,1,0:T(4,128)(2,1)} %param.9) | copy-start | bytes 4915204
  2.6 5.2 %copy-start.1 = (f32[16,32,648]{2,1,0:T(8,128)S(1)}, f32[16,32,648]{2,1,0:T(8,128)}, u32[]{:S(2)}) copy-start(f32[16,32,648]{2,1,0:T(8,128)} %spec_ref.1) | copy-start | bytes 3981316
  2.6 5.2 %copy-start.2 = (f32[2,16,648]{2,1,0:T(8,128)S(1)}, f32[2,16,648]{2,1,0:T(8,128)}, u32[]{:S(2)}) copy-start(f32[2,16,648]{2,1,0:T(8,128)} %constant.22.clone.cst_ref) | copy-start | bytes 248836
  2.6 5.2 %copy-start.3 = (s32[4,256]{1,0:T(4,128)S(1)}, s32[4,256]{1,0:T(4,128)}, u32[]{:S(2)}) copy-start(s32[4,256]{1,0:T(4,128)} %rs_ref.1) | copy-start | bytes 12292
  2.6 5.2 %copy-start.4 = (s32[32]{0:T(128)S(1)}, s32[32]{0:T(128)}, u32[]{:S(2)}) copy-start(s32[32]{0:T(128)} %cp_ref.1) | copy-start | bytes 388

commit v2 on v1

v2 whole, which is shorter than its diff:
```python
import math

import numpy as np

import jax
import jax.numpy as jnp
from jax import lax
from jax.experimental import pallas as pl
from jax.experimental.pallas import tpu as pltpu
from jax.sharding import PartitionSpec as P

LON = 4096
NDIR = 36
NFREQ = 36
F32 = jnp.float32
BF16 = jnp.bfloat16
MESH = pl.DeviceIdType.MESH

N_A = 8
N_B = 16
N_X = 4
N_Z = 4
WAVES = 640
BLOCK = WAVES // N_A
GROUPS = BLOCK // 8
NT = 1280
CYCLES = 4
SLOTS = LON // N_B
ROWS = 16
COLS = 32
HALF = NDIR * NFREQ // 2
POINTS = 128
TILES = [(j, min(128, HALF - j)) for j in range(0, HALF, 128)]


def bin_table():
    b = np.arange(NDIR * NFREQ)
    theta = 2 * np.pi * (b // NFREQ + 0.5) / NDIR
    ratio = np.exp(-math.log(1.1) * (b % NFREQ))
    freq = 0.04177 / ratio
    east = 0.45 * ratio * np.cos(theta)
    north = 0.45 * ratio * np.sin(theta)
    q = 2 * np.pi * freq / 9.81
    width = 0.1 * freq * (2 * np.pi / NDIR)
    rows = [
        np.abs(east),
        np.abs(north),
        1.0 - np.abs(east) - np.abs(north),
        np.sign(east),
        np.sign(north),
        10.0 * q * np.cos(theta),
        10.0 * q * np.sin(theta),
        width,
        0.5 * freq / 0.2,
    ]
    rows += [np.zeros_like(freq)] * (16 - len(rows))
    table = np.stack(rows).astype(np.float32)
    return np.stack([table[:, :HALF], table[:, HALF:]])


AE, AN, CC, SE, SN, QE, QN, WB, DF = range(9)


def poly(y2, coefs):
    acc = jnp.full_like(y2, coefs[-1])
    for c in coefs[-2::-1]:
        acc = acc * y2 + c
    return acc


SIN_C = [(-1.0) ** i / math.factorial(2 * i + 1) for i in range(7)]
COS_C = [(-1.0) ** i / math.factorial(2 * i) for i in range(7)]


def turn(mk, count, inv):
    rest = mk - jnp.floor(mk * inv + 0.5) * count
    y = (rest * inv) * math.pi
    y2 = y * y
    s = y * poly(y2, SIN_C)
    c = poly(y2, COS_C)
    return 1.0 - 2.0 * s * s, 2.0 * s * c


def rcopy(src, dst, send, recv, device):
    return pltpu.make_async_remote_copy(
        src_ref=src, dst_ref=dst, send_sem=send, recv_sem=recv, device_id=device, device_id_type=MESH
    )


def lanes(rows, width=128):
    return lax.broadcasted_iota(jnp.int32, (rows, width), 1)


def sublanes(rows, width=128):
    return lax.broadcasted_iota(jnp.int32, (rows, width), 0)


def spread(row, n):
    kept = jnp.where(sublanes(n, n) == lanes(n, n), jnp.broadcast_to(row, (n, n)), 0.0)
    return jnp.broadcast_to(jnp.sum(kept, axis=1, keepdims=True), (n, 128))


def one_hot(mask):
    return mask.astype(F32).astype(BF16)


def dot(x, y, dims=((1,), (0,))):
    return lax.dot_general(x, y, (dims, ((), ())), preferred_element_type=F32)


def kernel(
    cp_ref, leg_hbm, coef_hbm, spec_hbm, mask_hbm, wc_hbm, cst_hbm,
    gw_ref, ws_ref, rough,
    leg, coef, spec, mask_in, wc, cst_ref, sall, msg, a2a, a2x, gath, gperm, low_f, l0,
    table, ptable, ca, sa, buf_a, buf_b, d2, edge, edge_in,
    mask_b, east_b, north_b, part, part_in, st, st_in,
    i_sem, leg_sem, a_send, a_recv, x_send, x_recv, g_send, g_recv, l_send, l_recv, h_send, h_recv,
    c_send, c_recv, r_send, r_recv,
):
    s = lax.axis_index("comp")
    a = lax.axis_index("aa")
    b = lax.axis_index("ba")
    x, z = b // N_Z, b % N_Z
    partner = {"comp": 1 - s}

    coef_copy = pltpu.make_async_copy(coef_hbm, coef, i_sem.at[0])
    coef_copy.start()
    leg_copies = lambda g: pltpu.make_async_copy(
        leg_hbm.at[pl.ds(g * 8, 8)], leg.at[pl.ds(g * 8, 8)], leg_sem.at[g]
    )
    for g in range(GROUPS):
        leg_copies(g).start()
    small = [
        pltpu.make_async_copy(mask_hbm, mask_in, i_sem.at[1]),
        pltpu.make_async_copy(wc_hbm, wc, i_sem.at[2]),
        pltpu.make_async_copy(cst_hbm, cst_ref, i_sem.at[3]),
        pltpu.make_async_copy(spec_hbm, spec, i_sem.at[4]),
    ]
    for c in small:
        c.start()

    barrier = pltpu.get_barrier_semaphore()
    pl.semaphore_signal(barrier, inc=1, device_id=partner, device_id_type=MESH)
    for d in range(1, N_A):
        pl.semaphore_signal(barrier, inc=1, device_id={"aa": lax.rem(a + d, N_A)}, device_id_type=MESH)
    for d in range(1, N_B):
        pl.semaphore_signal(barrier, inc=1, device_id={"ba": lax.rem(b + d, N_B)}, device_id_type=MESH)

    @pl.when(b == 0)
    def _():
        for d in range(1, N_A):
            pl.semaphore_signal(
                barrier, inc=1, device_id={"comp": 1 - s, "aa": lax.rem(a + d, N_A)}, device_id_type=MESH
            )

    coef_copy.wait()

    def legendre(g, carry):
        rows = []
        for i in range(8):
            order = a * BLOCK + g * 8 + i
            block = jnp.concatenate([coef[g * 8 + i, p].astype(F32) for p in range(2)], axis=0)
            rows.append(jnp.where(lanes(8, NT) >= order, block, 0.0))
        rows = jnp.concatenate(rows, axis=0).astype(BF16)
        leg_copies(g).wait()
        cross = dot(rows, leg[pl.ds(g * 8, 8)].reshape(256, NT), ((1,), (1,)))
        at = pl.ds(pl.multiple_of(g * 8, 8), 8)
        for t in range(2):
            kept = cross[t * 32 : t * 32 + 8, t * 128 : t * 128 + 128]
            for q in range(1, 4):
                m = t * 4 + q
                kept = jnp.where(lanes(8) >= q * 32, cross[m * 8 : m * 8 + 8, t * 128 : t * 128 + 128], kept)
            sall[at, t * 128 : t * 128 + 128] = kept
        return carry

    lax.fori_loop(0, GROUPS, legendre, 0)

    i, o = sublanes(256, 256), lanes(256, 256)
    moved = dot(sall[...].astype(BF16), one_hot(o == (i & 31) // 4 * 32 + (i // 32) * 4 + (i & 3)))
    turned = {}
    for t in range(N_A):
        for q in range(3):
            acc = jnp.zeros((8, 128), F32)
            for g in range(q * 4, min(q * 4 + 4, GROUPS)):
                shift = 32 * ((g - t) % 4)
                key = (g, t // 4, shift)
                if key not in turned:
                    v = moved[g * 8 : g * 8 + 8, t // 4 * 128 : t // 4 * 128 + 128]
                    turned[key] = pltpu.roll(v, shift, axis=1) if shift else v
                at = lanes(8) // 32 == g % 4
                acc = jnp.where(at, turned[key], acc)
            msg[t, :, q * 128 : q * 128 + 128] = acc

    pl.semaphore_wait(barrier, N_A + N_B - 1 + jnp.where(b == 0, N_A - 1, 0))

    sent = []
    for d in range(1, N_A):
        t = lax.rem(a + d, N_A)
        c = rcopy(msg.at[t], a2a.at[a], a_send.at[d - 1], a_recv.at[a], {"aa": t})
        c.start()
        sent.append(c)
    crossed = []
    for d in range(N_A):
        t = lax.rem(a + d, N_A)
        crossed.append(
            rcopy(msg.at[t], a2x.at[a], x_send.at[d], x_recv.at[a], {"comp": 1 - s, "aa": t})
        )

    @pl.when(b == 0)
    def _():
        for c in crossed:
            c.start()

    a2a[a] = msg[a]

    for c in small:
        c.wait()
    sea = mask_in[...].astype(F32)
    for r in range(ROWS):
        mask_b[r * COLS : (r + 1) * COLS, :] = spread(sea[r : r + 1, :], COLS)

    def first(r, carry):
        m = mask_b[pl.ds(r * COLS, COLS), :]
        for j, w in TILES:
            v = spec[r, :, j : j + w] * m[:, :w]
            buf_a[r + 1, 8 : 8 + COLS, j : j + w] = v
            edge[0, 0, r, :, j : j + w] = v[0:1, :]
            edge[0, 1, r, :, j : j + w] = v[COLS - 1 : COLS, :]
        return carry

    lax.fori_loop(0, ROWS, first, 0)

    def halo(buf, step):
        return [
            (a < N_A - 1, a > 0, rcopy(
                buf.at[ROWS, pl.ds(8, COLS)], buf.at[0, pl.ds(8, COLS)],
                h_send.at[step, 0], h_recv.at[step, 0], {"aa": lax.rem(a + 1, N_A)})),
            (a > 0, a < N_A - 1, rcopy(
                buf.at[1, pl.ds(8, COLS)], buf.at[ROWS + 1, pl.ds(8, COLS)],
                h_send.at[step, 1], h_recv.at[step, 1], {"aa": lax.rem(a + N_A - 1, N_A)})),
            (b < N_B - 1, b > 0, rcopy(
                edge.at[step, 1], edge_in.at[step, 0],
                h_send.at[step, 2], h_recv.at[step, 2], {"ba": lax.rem(b + 1, N_B)})),
            (b > 0, b < N_B - 1, rcopy(
                edge.at[step, 0], edge_in.at[step, 1],
                h_send.at[step, 3], h_recv.at[step, 3], {"ba": lax.rem(b + N_B - 1, N_B)})),
        ]

    def halo_start(copies):
        for can, _, c in copies:
            pl.when(can)(c.start)

    def halo_land(copies, buf, step):
        for i, (_, comes, c) in enumerate(copies):
            pl.when(comes)(c.wait_recv)

            @pl.when(jnp.logical_not(comes))
            def _():
                if i < 2:
                    buf[0 if i == 0 else ROWS + 1, 8 : 8 + COLS, :] = jnp.zeros((COLS, HALF), F32)
                else:
                    edge_in[step, i - 2] = jnp.zeros((ROWS, 1, HALF), F32)

        for r in range(ROWS):
            buf[r + 1, 7:8, :] = edge_in[step, 0, r]
            buf[r + 1, 8 + COLS : 9 + COLS, :] = edge_in[step, 1, r]

    def halo_sent(copies):
        for can, _, c in copies:
            pl.when(can)(c.wait_send)

    halo_a = halo(buf_a, 0)
    halo_start(halo_a)

    def tables(out, l, k, active):
        w = k.shape[1]
        count = jnp.full((1, w), cp_ref[a * CYCLES + l], jnp.int32).astype(F32)
        inv = 1.0 / count
        cu, su = turn(sublanes(WAVES // 8, w).astype(F32) * 8.0 * k, count, inv)
        ca[:, :, :w] = cu.reshape(GROUPS, 8, w)
        sa[:, :, :w] = su.reshape(GROUPS, 8, w)
        cv, sv = turn(sublanes(8, w).astype(F32) * k, count, inv)
        cv, sv = cv * active, sv * active
        minus_c, minus_s = -cv, -sv

        def block(i, carry):
            for h in range(4):
                cs, ss = [], []
                for o in range(h * 2, h * 2 + 2):
                    c0, s0 = ca[i, o : o + 1, :w], sa[i, o : o + 1, :w]
                    cs.append(c0 * cv + s0 * minus_s)
                    ss.append(s0 * minus_c + c0 * minus_s)
                at = pl.multiple_of(i * 64 + h * 16, 16)
                out[l, pl.ds(at, 16), :] = jnp.concatenate(cs, axis=0).astype(BF16)
                out[l, pl.ds(WAVES + at, 16), :] = jnp.concatenate(ss, axis=0).astype(BF16)
            return carry

        lax.fori_loop(0, GROUPS, block, 0)
        top = out[l, 0:16, :].astype(F32)
        out[l, 0:16, :] = jnp.where(sublanes(16, w) == 0, top * 0.5, top).astype(BF16)

    near = wc[:, pl.ds(pl.multiple_of(b // 4 * 128, 128), 128)].astype(F32)
    near = pltpu.roll(near, (4 - b % 4) % 4 * COLS, axis=1)
    near = jnp.where(lanes(ROWS) < COLS, near, 0.0)
    side = near
    for q in range(1, 4):
        side = jnp.where(sublanes(ROWS) % 4 == q, pltpu.roll(near, q * COLS, axis=1), side)
    for l in range(CYCLES):
        tables(ptable, l, jnp.sum(side[l * 4 : l * 4 + 4, :], axis=0, keepdims=True), 2.0)

    i, o = sublanes(384, 512), lanes(384, 512)
    order = one_hot((o == (i & 3) * 128 + i // 4) & (i < BLOCK * 4))

    def compact(landed):
        wide = dot(landed[...].reshape(64, 384).astype(BF16), order)
        out = []
        for l in range(CYCLES):
            tiles = [jnp.zeros((8, 128), F32) for _ in range(WAVES // 128)]
            for c in range(N_A):
                t, shift = divmod(c * BLOCK, 128)
                piece = wide[c * 8 : c * 8 + 8, l * 128 : l * 128 + 128]
                if shift:
                    piece = pltpu.roll(piece, shift, axis=1)
                    tiles[t] = jnp.where(lanes(8) >= shift, piece, tiles[t])
                    if shift + BLOCK > 128:
                        tiles[t + 1] = jnp.where(lanes(8) < shift, piece, tiles[t + 1])
                else:
                    tiles[t] = jnp.where(lanes(8) < BLOCK, piece, tiles[t])
            out.append(tiles)
        return out

    def lowest(blocks, base):
        for l in range(CYCLES):
            for t in range(WAVES // 128):
                for p in range(2):
                    r = base + p * 4 + l
                    low_f[r : r + 1, t * 128 : t * 128 + 128] = blocks[l][t][p * 4 : p * 4 + 1, :]

    for d in range(1, N_A):
        c = lax.rem(a + N_A - d, N_A)
        rcopy(msg.at[0], a2a.at[c], a_send.at[d - 1], a_recv.at[c], {"aa": c}).wait_recv()
    blocks = compact(a2a)
    low = [
        rcopy(l0, l0, l_send.at[d - 1], l_recv.at[0], {"ba": lax.rem(b + d, N_B)}) for d in range(1, N_B)
    ]

    @pl.when(b == 0)
    def _():
        lowest(blocks, 0)
        for d in range(N_A):
            c = lax.rem(a + N_A - d, N_A)
            rcopy(msg.at[0], a2x.at[c], x_send.at[d], x_recv.at[c], {"comp": 1 - s, "aa": c}).wait_recv()
        lowest(compact(a2x), 8)
        l0[...] = low_f[...].astype(BF16)
        for c in low:
            c.start()

    for t in range(WAVES // 128):
        up = [pltpu.roll(blocks[l][t], 4, axis=0) for l in range(CYCLES)]
        own = [blocks[l][t] for l in range(CYCLES)]
        top = sublanes(8) < 4
        for p in range(2):
            pair = [
                jnp.where(top, own[l], up[l + 1]) if p == 0 else jnp.where(top, up[l], own[l + 1])
                for l in (0, 2)
            ]
            at = p * WAVES + t * 128
            gath[b, :, at : at + 128] = jnp.concatenate(pair, axis=0).astype(BF16)

    gathers = []

    def give(o, device):
        c = rcopy(gath.at[o], gath.at[o], g_send.at[len(gathers)], g_recv.at[o], {"ba": device})
        c.start()
        gathers.append(c)

    def arrived(o):
        rcopy(gath.at[o], gath.at[o], g_send.at[0], g_recv.at[o], {"ba": o}).wait_recv()

    x_peers = [lax.rem(x + d, N_X) * N_Z + z for d in (1, 3, 2)]
    for d in range(1, N_Z):
        give(b, x * N_Z + lax.rem(z + d, N_Z))
    for t in x_peers:
        give(b, t)

    def upwind(buf, r, j, w):
        c = lambda i: cst_ref[s, i : i + 1, j : j + w]
        here = buf[r + 1, 8 : 8 + COLS, j : j + w]
        ux = jnp.where(c(SE) > 0.0, buf[r + 1, 7 : 7 + COLS, j : j + w], buf[r + 1, 9 : 9 + COLS, j : j + w])
        uy = jnp.where(c(SN) > 0.0, buf[r, 8 : 8 + COLS, j : j + w], buf[r + 2, 8 : 8 + COLS, j : j + w])
        return here * c(CC) + ux * c(AE) + uy * c(AN)

    halo_land(halo_a, buf_a, 0)

    def second(r, carry):
        m = mask_b[pl.ds(r * COLS, COLS), :]
        for j, w in TILES:
            v = upwind(buf_a, r, j, w) * m[:, :w]
            buf_b[r + 1, 8 : 8 + COLS, j : j + w] = v
            edge[1, 0, r, :, j : j + w] = v[0:1, :]
            edge[1, 1, r, :, j : j + w] = v[COLS - 1 : COLS, :]
        return carry

    lax.fori_loop(0, ROWS, second, 0)
    halo_b = halo(buf_b, 1)
    halo_start(halo_b)

    for d in range(1, N_Z):
        o = x * N_Z + lax.rem(z + N_Z - d, N_Z)
        arrived(o)
        for t in x_peers:
            give(o, t)

    halo_land(halo_b, buf_b, 1)

    def third(r, carry):
        at = pl.ds(r * COLS, COLS)
        m = mask_b[at, :]
        total = jnp.zeros((COLS, 128), F32)
        for j, w in TILES:
            v = upwind(buf_b, r, j, w) * m[:, :w]
            d2[r, :, j : j + w] = v
            term = v * cst_ref[s, WB : WB + 1, j : j + w]
            if w == 128:
                total = total + term
            else:
                part[0, at, :] = total
                part[0, at, :w] = total[:, :w] + term
        return carry

    lax.fori_loop(0, ROWS, third, 0)
    energy_copy = rcopy(part.at[0], part_in, c_send.at[0], c_recv.at[0], partner)
    energy_copy.start()

    @pl.when(b > 0)
    def _():
        low[0].wait_recv()

    own, other = [], []
    for l in range(CYCLES):
        pc = dot(l0[...], ptable[l, 0:WAVES, :])
        ps = dot(l0[...], ptable[l, WAVES:, :])
        own.append((pc[l : l + 1, :] + ps[4 + l : 5 + l, :]).astype(BF16).astype(F32))
        other.append((pc[8 + l : 9 + l, :] + ps[12 + l : 13 + l, :]).astype(BF16).astype(F32))
    east = [jnp.where(s == 0, p, q) for p, q in zip(own, other)]
    north = [jnp.where(s == 0, q, p) for p, q in zip(own, other)]
    for l in range(CYCLES):
        east_b[pl.ds(l * POINTS, POINTS), :] = spread(east[l], POINTS)
        north_b[pl.ds(l * POINTS, POINTS), :] = spread(north[l], POINTS)

    def gain_of(e, n, r, j, w):
        c = lambda i: cst_ref[s, i : i + 1, j : j + w]
        align = e[:, :w] * c(QE) + n[:, :w] * c(QN)
        grown = 0.05 * jnp.maximum(align - 1.0, 0.0) * d2[r, :, j : j + w]
        return align, grown

    def fourth(r, carry):
        at = pl.ds(r * COLS, COLS)
        e, n = east_b[at, :], north_b[at, :]
        total = jnp.zeros((COLS, 128), F32)
        for j, w in TILES:
            align, grown = gain_of(e, n, r, j, w)
            term = grown * align * cst_ref[s, WB : WB + 1, j : j + w]
            if w == 128:
                total = total + term
            else:
                part[1, at, :] = total
                part[1, at, :w] = total[:, :w] + term
        return carry

    lax.fori_loop(0, ROWS, fourth, 0)
    for l in range(CYCLES):
        total = jnp.sum(part[1, pl.ds(l * POINTS, POINTS), :], axis=1, keepdims=True)
        kept = jnp.where(sublanes(POINTS) == lanes(POINTS), jnp.broadcast_to(total, (POINTS, 128)), 0.0)
        row = jnp.sum(kept, axis=0, keepdims=True)
        st[l : l + 1, :] = row
        st[4 + l : 5 + l, :] = row
    stress_copy = rcopy(st, st_in, c_send.at[1], c_recv.at[1], partner)
    stress_copy.start()

    energy_copy.wait_recv()
    for l in range(CYCLES):
        at = pl.ds(l * POINTS, POINTS)
        level = jnp.sum(part[0, at, :] + part_in[at, :], axis=1, keepdims=True) * 0.125
        mask_b[at, :] = jnp.broadcast_to(level * level, (POINTS, 128))

    def fifth(r, carry):
        at = pl.ds(r * COLS, COLS)
        e, n = east_b[at, :], north_b[at, :]
        square = mask_b[at, :]
        for j, w in TILES:
            _, grown = gain_of(e, n, r, j, w)
            decay = square[:, :w] * cst_ref[s, DF : DF + 1, j : j + w]
            ws_ref[r, :, j : j + w] = (d2[r, :, j : j + w] + grown) / (1.0 + decay)
        return carry

    lax.fori_loop(0, ROWS, fifth, 0)

    stress_copy.wait_recv()
    e, n = jnp.concatenate(east * 2, axis=0), jnp.concatenate(north * 2, axis=0)
    air = 0.12 * (e * e + n * n) + 0.02
    rough[b] = jnp.sqrt(1.0 + 0.03 * (st[...] + st_in[...]) / air)
    rough_copies = []
    for d in range(1, N_B):
        t = lax.rem(b + d, N_B)
        c = rcopy(rough.at[b], rough.at[b], r_send.at[d - 1], r_recv.at[b], {"ba": t})
        c.start()
        rough_copies.append(c)

    slots = lanes(1, SLOTS) + b * SLOTS
    for l in range(CYCLES):
        active = jnp.where(slots < cp_ref[a * CYCLES + l], 2.0, 0.0)
        tables(table, l, slots.astype(F32), active)
    for xd in range(1, N_X):
        for zd in range(N_Z):
            arrived(lax.rem(x + N_X - xd, N_X) * N_Z + lax.rem(z + zd, N_Z))
    r = sublanes(256, 256)
    order = one_hot(lanes(256, 256) == (r & 63) // 4 * 16 + r // 64 * 4 + (r & 3))
    for k in range(0, 2 * WAVES, 256):
        gperm[:, k : k + 256] = dot(order, gath[:, :, k : k + 256].reshape(256, 256)).astype(BF16)
    for l in range(CYCLES):
        gw_ref[0, l] = dot(gperm[l * 64 : l * 64 + 64, :], table[l]).astype(BF16)

    for d in range(1, N_B):
        o = lax.rem(b + N_B - d, N_B)
        rcopy(rough.at[o], rough.at[o], r_send.at[0], r_recv.at[o], {"ba": o}).wait_recv()
    for c in sent + gathers + rough_copies + [energy_copy, stress_copy]:
        c.wait_send()
    halo_sent(halo_a)
    halo_sent(halo_b)

    @pl.when(b == 0)
    def _():
        for c in low + crossed:
            c.wait_send()


def last(cp_ref, gw_in, ws_in, rough, rs_ref, gw_ref, ws_ref, ch_ref, sem):
    a = lax.axis_index("aa")
    slots = lanes(1, SLOTS) + lax.axis_index("ba") * SLOTS
    copies = [
        pltpu.make_async_copy(ws_in, ws_ref, sem.at[0]),
        pltpu.make_async_copy(gw_in, gw_ref, sem.at[1]),
    ]
    for c in copies:
        c.start()
    for l in range(CYCLES):
        source = rs_ref[l : l + 1, :]
        low_part = ((source >> 9) & 3) * 32 + (source & 31)
        high_part = (source >> 5) & 15
        pick = one_hot(sublanes(128, SLOTS) == low_part)
        values = rough[:, l, :]
        h0 = values.astype(BF16)
        r1 = values - h0.astype(F32)
        h1 = r1.astype(BF16)
        h2 = (r1 - h1.astype(F32)).astype(BF16)
        got = dot(h0, pick) + (dot(h1, pick) + dot(h2, pick))
        keep = sublanes(N_B, SLOTS) == high_part
        row = jnp.sum(jnp.where(keep, got, 0.0), axis=0, keepdims=True)
        ch_ref[l : l + 1, :] = jnp.where(slots < cp_ref[a * CYCLES + l], row, 0.0)
    for c in copies:
        c.wait()


def per_device(legendre, coefficients, cycle_points, spectra, sea_mask, wind_column, roughness_source):
    vmem = pl.BlockSpec(memory_space=pltpu.VMEM)
    smem = pl.BlockSpec(memory_space=pltpu.SMEM)
    hbm = pl.BlockSpec(memory_space=pl.ANY)
    dma = pltpu.SemaphoreType.DMA
    winds = jax.ShapeDtypeStruct((1, CYCLES, 64, SLOTS), BF16)
    waves = jax.ShapeDtypeStruct((ROWS, COLS, HALF), F32)
    winds_done, waves_done, rough = pl.pallas_call(
        kernel,
        out_shape=(winds, waves, jax.ShapeDtypeStruct((N_B, 8, 128), F32)),
        in_specs=[smem] + [hbm] * 6,
        out_specs=(vmem, vmem, vmem),
        scratch_shapes=[
            pltpu.VMEM((BLOCK, 32, NT), BF16),
            pltpu.VMEM((BLOCK, 2, 4, NT), BF16),
            pltpu.VMEM((ROWS, COLS, HALF), F32),
            pltpu.VMEM((ROWS, COLS), jnp.int32),
            pltpu.VMEM((ROWS, 512), jnp.int32),
            pltpu.VMEM((2, 16, HALF), F32),
            pltpu.VMEM((BLOCK, 256), F32),
            pltpu.VMEM((N_A, 8, 384), F32),
            pltpu.VMEM((N_A, 8, 384), F32),
            pltpu.VMEM((N_A, 8, 384), F32),
            pltpu.VMEM((N_B, 16, 2 * WAVES), BF16),
            pltpu.VMEM((256, 2 * WAVES), BF16),
            pltpu.VMEM((16, WAVES), F32),
            pltpu.VMEM((16, WAVES), BF16),
            pltpu.VMEM((CYCLES, 2 * WAVES, SLOTS), BF16),
            pltpu.VMEM((CYCLES, 2 * WAVES, POINTS), BF16),
            pltpu.VMEM((GROUPS, 8, SLOTS), F32),
            pltpu.VMEM((GROUPS, 8, SLOTS), F32),
            pltpu.VMEM((ROWS + 2, COLS + 16, HALF), F32),
            pltpu.VMEM((ROWS + 2, COLS + 16, HALF), F32),
            pltpu.VMEM((ROWS, COLS, HALF), F32),
            pltpu.VMEM((2, 2, ROWS, 1, HALF), F32),
            pltpu.VMEM((2, 2, ROWS, 1, HALF), F32),
            pltpu.VMEM((ROWS * COLS, 128), F32),
            pltpu.VMEM((ROWS * COLS, 128), F32),
            pltpu.VMEM((ROWS * COLS, 128), F32),
            pltpu.VMEM((2, ROWS * COLS, 128), F32),
            pltpu.VMEM((ROWS * COLS, 128), F32),
            pltpu.VMEM((8, 128), F32),
            pltpu.VMEM((8, 128), F32),
            dma((5,)), dma((GROUPS,)),
            dma((N_A - 1,)), dma((N_A,)),
            dma((N_A,)), dma((N_A,)),
            dma((N_B - 1,)), dma((N_B,)),
            dma((N_B - 1,)), dma((1,)),
            dma((2, 4)), dma((2, 4)),
            dma((2,)), dma((2,)),
            dma((N_B - 1,)), dma((N_B,)),
        ],
        compiler_params=pltpu.CompilerParams(
            collective_id=0, has_side_effects=True, vmem_limit_bytes=50 * 1024 * 1024
        ),
    )(
        cycle_points, legendre, coefficients.reshape(BLOCK, 2, 4, NT), spectra, sea_mask, wind_column,
        jnp.asarray(bin_table()),
    )
    return pl.pallas_call(
        last,
        out_shape=(winds, waves, jax.ShapeDtypeStruct((CYCLES, SLOTS), F32)),
        in_specs=[smem, vmem, vmem, vmem, vmem],
        out_specs=(hbm, hbm, vmem),
        scratch_shapes=[dma((2,))],
    )(cycle_points, winds_done, waves_done, rough, roughness_source)


def solution(mesh):
    in_specs = (
        P("aa", None, None),
        P("comp", "aa", None, "ba", None),
        P(),
        P("aa", "ba", "comp"),
        P("aa", "ba"),
        P("aa", None),
        P("aa", "ba"),
    )
    out_specs = (P("comp", "aa", None, "ba"), P("aa", "ba", "comp"), P("aa", "ba"))
    return jax.shard_map(
        per_device, mesh=mesh, in_specs=in_specs, out_specs=out_specs, check_vma=False
    )
```

time: 52.1 us -> 54.4 us (1.044)
  Pallas kernels: 41.1 us -> 46.6 us
  matrix products: 4.79 us -> 0 us
  local copies, waits for them, and re-layouts: 4.52 us -> 6.82 us
    pallas_call x1 -> x2, Pallas kernels: 41.1 us -> 46.6 us  [the longest x1 43.4 us: per_device(): pl.pallas_call(kernel, out_shape=(winds, waves, jax.ShapeDtypeStruct((N_B...]
    dot_general x1 -> x0, matrix products: 4.79 us -> none  [per_device(): jnp.einsum('mln,mpcn->mlpc', masked, coefficients[0], preferred_element_t...]
    unnamed x14 -> x16, local copies, waits for them, and re-layouts: 2.5 us -> 6.82 us
    reshape x3 -> x0, local copies, waits for them, and re-layouts: 1.02 us -> none  [the longest x1 0.89 us: per_device(): sea_mask.reshape(4, POINTS)]
    dynamic_slice x1 -> x0, local copies, waits for them, and re-layouts: 0.77 us -> none  [per_device(): own = lax.dynamic_slice_in_dim(wind_column, column * COLS, COLS, 1)]
where the time goes in v2:
time: 54.4 us; the launch traced here: 54.1 us
  Pallas kernels  46.6 us (86%)
  local copies, waits for them, and re-layouts  6.82 us (13%)
  between operations  0.66 us (1%)
    pallas_call x1, Pallas kernels, per_device(): pl.pallas_call(kernel, out_shape=(winds, waves, jax.ShapeDtypeStruct((N_B...  43.4 us
    unnamed x16, local copies, waits for them, and re-layouts  6.82 us
    pallas_call x1, Pallas kernels, per_device(): pl.pallas_call(last, out_shape=(winds, waves, jax.ShapeDtypeStruct((CYCLE...  3.2 us

profile of v2, /device:TPU:1, one launch (start us, length us, event | category | flops | bytes accessed | tf_op | source)
XLA Modules:
  0.0 54.1 jit_solution(60428666807119774)
XLA Ops:
  0.6 0.0 copy-start.1
  0.6 1.4 %copy-done.1 = f32[16,32,648]{2,1,0:T(8,128)S(1)} copy-done((f32[16,32,648]{2,1,0:T(8,128)S(1)}, f32[16,32,648]{2,1,0:T(8,128)}, u32[]{:S(2)}) %copy-start.1) | copy-done | bytes 1327128
  2.0 0.0 copy-start.3
  2.0 0.9 %copy-done.3 = f32[2,16,648]{2,1,0:T(8,128)S(1)} copy-done((f32[2,16,648]{2,1,0:T(8,128)S(1)}, f32[2,16,648]{2,1,0:T(8,128)}, u32[]{:S(2)}) %copy-start.3) | copy-done | bytes 82968
  2.9 0.0 copy-start.5
  2.9 0.8 %copy-done.5 = s32[16,512]{1,0:T(8,128)S(1)} copy-done((s32[16,512]{1,0:T(8,128)S(1)}, s32[16,512]{1,0:T(8,128)}, u32[]{:S(2)}) %copy-start.5) | copy-done | bytes 32792
  3.7 0.0 copy-start.6
  3.7 0.7 %copy-done.6 = s32[16,32]{1,0:T(8,128)S(1)} copy-done((s32[16,32]{1,0:T(8,128)S(1)}, s32[16,32]{1,0:T(8,128)}, u32[]{:S(2)}) %copy-start.6) | copy-done | bytes 2072
  4.4 0.0 copy-start.7
  4.4 0.7 %copy-done.7 = s32[32]{0:T(128)S(1)} copy-done((s32[32]{0:T(128)S(1)}, s32[32]{0:T(128)}, u32[]{:S(2)}) %copy-start.7) | copy-done | bytes 152
  5.0 43.4 %shard_map.103 = (bf16[1,4,64,256]{3,2,1,0:T(8,128)(2,1)S(1)}, f32[16,32,648]{2,1,0:T(8,128)S(1)}, f32[16,8,128]{2,1,0:T(8,128)S(1)}) custom-call(s32[32]{0:T(128)S(1)} %copy-done.7, bf16[80,32,1280]{2,1,0:T(8,128)(2,1)} %leg_hbm.1, bf16[80,2,4,1280]{3,2,1,0:T(4,128)(2,1)} %bitcast.1, f32[16,32,648]{2,1,0:T(8,128)S(1)} %copy-done.1, s32[16,32]{1,0:T(8,128)S(1)} %copy-done.6, ...), custom_call_target="tpu_custom_call" | custom-call | tf_op jit(solution)/shard_map/pallas_call | solution.py:572
  48.4 0.0 copy-start
  48.4 1.1 %copy-done = f32[16,32,648]{2,1,0:T(8,128)} copy-done((f32[16,32,648]{2,1,0:T(8,128)}, f32[16,32,648]{2,1,0:T(8,128)S(1)}, u32[]{:S(2)}) %copy-start) | copy-done | bytes 1327128
  49.6 0.0 copy-start.2
  49.6 0.7 %copy-done.2 = bf16[1,4,64,256]{3,2,1,0:T(8,128)(2,1)} copy-done((bf16[1,4,64,256]{3,2,1,0:T(8,128)(2,1)}, bf16[1,4,64,256]{3,2,1,0:T(8,128)(2,1)S(1)}, u32[]{:S(2)}) %copy-start.2) | copy-done | bytes 131096
  50.2 0.0 copy-start.4
  50.2 0.6 %copy-done.4 = f32[16,8,128]{2,1,0:T(8,128)} copy-done((f32[16,8,128]{2,1,0:T(8,128)}, f32[16,8,128]{2,1,0:T(8,128)S(1)}, u32[]{:S(2)}) %copy-start.4) | copy-done | bytes 65560
  50.9 3.2 %shard_map.104 = (bf16[1,4,64,256]{3,2,1,0:T(8,128)(2,1)}, f32[16,32,648]{2,1,0:T(8,128)}, f32[4,256]{1,0:T(4,128)}) custom-call(s32[32]{0:T(128)} %cp_ref.3, bf16[1,4,64,256]{3,2,1,0:T(8,128)(2,1)} %copy-done.2, f32[16,32,648]{2,1,0:T(8,128)} %copy-done, f32[16,8,128]{2,1,0:T(8,128)} %copy-done.4, s32[4,256]{1,0:T(4,128)} %rs_ref.1), custom_call_target="tpu_custom_call" | custom-call | tf_op jit(solution)/shard_map/pallas_call | solution.py:624
Async XLA Ops:
  0.6 1.4 %copy-start.1 = (f32[16,32,648]{2,1,0:T(8,128)S(1)}, f32[16,32,648]{2,1,0:T(8,128)}, u32[]{:S(2)}) copy-start(f32[16,32,648]{2,1,0:T(8,128)} %spec_hbm.1) | copy-start | bytes 3981316
  2.0 0.9 %copy-start.3 = (f32[2,16,648]{2,1,0:T(8,128)S(1)}, f32[2,16,648]{2,1,0:T(8,128)}, u32[]{:S(2)}) copy-start(f32[2,16,648]{2,1,0:T(8,128)} %constant.2.clone.cst_hbm) | copy-start | bytes 248836
  2.9 0.8 %copy-start.5 = (s32[16,512]{1,0:T(8,128)S(1)}, s32[16,512]{1,0:T(8,128)}, u32[]{:S(2)}) copy-start(s32[16,512]{1,0:T(8,128)} %wc_hbm.1) | copy-start | bytes 98308
  3.7 0.7 %copy-start.6 = (s32[16,32]{1,0:T(8,128)S(1)}, s32[16,32]{1,0:T(8,128)}, u32[]{:S(2)}) copy-start(s32[16,32]{1,0:T(8,128)} %mask_hbm.1) | copy-start | bytes 6148
  4.4 0.7 %copy-start.7 = (s32[32]{0:T(128)S(1)}, s32[32]{0:T(128)}, u32[]{:S(2)}) copy-start(s32[32]{0:T(128)} %cp_ref.3) | copy-start | bytes 388
  48.4 1.1 %copy-start = (f32[16,32,648]{2,1,0:T(8,128)}, f32[16,32,648]{2,1,0:T(8,128)S(1)}, u32[]{:S(2)}) copy-start(f32[16,32,648]{2,1,0:T(8,128)S(1)} %get-tuple-element.7.ws_in) | copy-start | bytes 3981316
  49.6 0.7 %copy-start.2 = (bf16[1,4,64,256]{3,2,1,0:T(8,128)(2,1)}, bf16[1,4,64,256]{3,2,1,0:T(8,128)(2,1)S(1)}, u32[]{:S(2)}) copy-start(bf16[1,4,64,256]{3,2,1,0:T(8,128)(2,1)S(1)} %get-tuple-element.6.gw_in) | copy-start | bytes 393220
  50.2 0.6 %copy-start.4 = (f32[16,8,128]{2,1,0:T(8,128)}, f32[16,8,128]{2,1,0:T(8,128)S(1)}, u32[]{:S(2)}) copy-start(f32[16,8,128]{2,1,0:T(8,128)S(1)} %get-tuple-element.8.rough) | copy-start | bytes 196612

commit v3 on v2

--- a/solution.py
+++ b/solution.py
@@ -28,6 +28,7 @@
 SLOTS = LON // N_B
 ROWS = 16
 COLS = 32
+VMEM = 64_000_000
 HALF = NDIR * NFREQ // 2
 POINTS = 128
 TILES = [(j, min(128, HALF - j)) for j in range(0, HALF, 128)]
@@ -109,13 +110,13 @@
 
 
 def kernel(
-    cp_ref, leg_hbm, coef_hbm, spec_hbm, mask_hbm, wc_hbm, cst_hbm,
-    gw_ref, ws_ref, rough,
-    leg, coef, spec, mask_in, wc, cst_ref, sall, msg, a2a, a2x, gath, gperm, low_f, l0,
+    cp_hbm, leg_hbm, coef_hbm, spec_hbm, mask_hbm, wc_hbm, cst_hbm,
+    gw_out, ws_out, rough_out,
+    gw_ref, ws_ref, rough, cp_ref, leg, coef, spec, mask_in, wc, cst_ref, sall, msg, a2a, a2x, gath, gperm, low_f, l0,
     table, ptable, ca, sa, buf_a, buf_b, d2, edge, edge_in,
     mask_b, east_b, north_b, part, part_in, st, st_in,
     i_sem, leg_sem, a_send, a_recv, x_send, x_recv, g_send, g_recv, l_send, l_recv, h_send, h_recv,
-    c_send, c_recv, r_send, r_recv,
+    c_send, c_recv, r_send, r_recv, o_sem,
 ):
     s = lax.axis_index("comp")
     a = lax.axis_index("aa")
@@ -135,6 +136,7 @@
         pltpu.make_async_copy(wc_hbm, wc, i_sem.at[2]),
         pltpu.make_async_copy(cst_hbm, cst_ref, i_sem.at[3]),
         pltpu.make_async_copy(spec_hbm, spec, i_sem.at[4]),
+        pltpu.make_async_copy(cp_hbm, cp_ref, i_sem.at[5]),
     ]
     for c in small:
         c.start()
@@ -495,6 +497,8 @@
         return carry
 
     lax.fori_loop(0, ROWS, fifth, 0)
+    ws_copy = pltpu.make_async_copy(ws_ref, ws_out, o_sem.at[0])
+    ws_copy.start()
 
     stress_copy.wait_recv()
     e, n = jnp.concatenate(east * 2, axis=0), jnp.concatenate(north * 2, axis=0)
@@ -520,10 +524,14 @@
         gperm[:, k : k + 256] = dot(order, gath[:, :, k : k + 256].reshape(256, 256)).astype(BF16)
     for l in range(CYCLES):
         gw_ref[0, l] = dot(gperm[l * 64 : l * 64 + 64, :], table[l]).astype(BF16)
+    gw_copy = pltpu.make_async_copy(gw_ref, gw_out, o_sem.at[1])
+    gw_copy.start()
 
     for d in range(1, N_B):
         o = lax.rem(b + N_B - d, N_B)
         rcopy(rough.at[o], rough.at[o], r_send.at[0], r_recv.at[o], {"ba": o}).wait_recv()
+    rough_copy = pltpu.make_async_copy(rough, rough_out, o_sem.at[2])
+    rough_copy.start()
     for c in sent + gathers + rough_copies + [energy_copy, stress_copy]:
         c.wait_send()
     halo_sent(halo_a)
@@ -534,16 +542,27 @@
         for c in low + crossed:
             c.wait_send()
 
-
-def last(cp_ref, gw_in, ws_in, rough, rs_ref, gw_ref, ws_ref, ch_ref, sem):
+    for c in (ws_copy, gw_copy, rough_copy):
+        c.wait()
+
+
+def last(cp_hbm, gw_in, ws_in, rough, rs_ref, gw_ref, ws_ref, ch_ref, cp_ref, gw, ws, sem_in, sem_out):
     a = lax.axis_index("aa")
     slots = lanes(1, SLOTS) + lax.axis_index("ba") * SLOTS
-    copies = [
-        pltpu.make_async_copy(ws_in, ws_ref, sem.at[0]),
-        pltpu.make_async_copy(gw_in, gw_ref, sem.at[1]),
-    ]
-    for c in copies:
+    step = ROWS // 4
+    blocks = [pl.ds(i * step, step) for i in range(4)]
+    counts = pltpu.make_async_copy(cp_hbm, cp_ref, sem_in.at[5])
+    come = [pltpu.make_async_copy(ws_in.at[k], ws.at[k], sem_in.at[i]) for i, k in enumerate(blocks)]
+    come.append(pltpu.make_async_copy(gw_in, gw, sem_in.at[4]))
+    go = [pltpu.make_async_copy(ws.at[k], ws_ref.at[k], sem_out.at[i]) for i, k in enumerate(blocks)]
+    go.append(pltpu.make_async_copy(gw, gw_ref, sem_out.at[4]))
+    counts.start()
+    for c in come:
         c.start()
+    for c, d in zip(come, go):
+        c.wait()
+        d.start()
+    counts.wait()
     for l in range(CYCLES):
         source = rs_ref[l : l + 1, :]
         low_part = ((source >> 9) & 3) * 32 + (source & 31)
@@ -558,23 +577,27 @@
         keep = sublanes(N_B, SLOTS) == high_part
         row = jnp.sum(jnp.where(keep, got, 0.0), axis=0, keepdims=True)
         ch_ref[l : l + 1, :] = jnp.where(slots < cp_ref[a * CYCLES + l], row, 0.0)
-    for c in copies:
+    for c in go:
         c.wait()
 
 
 def per_device(legendre, coefficients, cycle_points, spectra, sea_mask, wind_column, roughness_source):
     vmem = pl.BlockSpec(memory_space=pltpu.VMEM)
     smem = pl.BlockSpec(memory_space=pltpu.SMEM)
-    hbm = pl.BlockSpec(memory_space=pl.ANY)
+    hbm = pl.BlockSpec(memory_space=pltpu.HBM)
     dma = pltpu.SemaphoreType.DMA
     winds = jax.ShapeDtypeStruct((1, CYCLES, 64, SLOTS), BF16)
     waves = jax.ShapeDtypeStruct((ROWS, COLS, HALF), F32)
     winds_done, waves_done, rough = pl.pallas_call(
         kernel,
         out_shape=(winds, waves, jax.ShapeDtypeStruct((N_B, 8, 128), F32)),
-        in_specs=[smem] + [hbm] * 6,
-        out_specs=(vmem, vmem, vmem),
+        in_specs=[hbm] * 7,
+        out_specs=(hbm, hbm, hbm),
         scratch_shapes=[
+            pltpu.VMEM((1, CYCLES, 64, SLOTS), BF16),
+            pltpu.VMEM((ROWS, COLS, HALF), F32),
+            pltpu.VMEM((N_B, 8, 128), F32),
+            pltpu.SMEM((32,), jnp.int32),
             pltpu.VMEM((BLOCK, 32, NT), BF16),
             pltpu.VMEM((BLOCK, 2, 4, NT), BF16),
             pltpu.VMEM((ROWS, COLS, HALF), F32),
@@ -605,7 +628,7 @@
             pltpu.VMEM((ROWS * COLS, 128), F32),
             pltpu.VMEM((8, 128), F32),
             pltpu.VMEM((8, 128), F32),
-            dma((5,)), dma((GROUPS,)),
+            dma((6,)), dma((GROUPS,)),
             dma((N_A - 1,)), dma((N_A,)),
             dma((N_A,)), dma((N_A,)),
             dma((N_B - 1,)), dma((N_B,)),
@@ -613,9 +636,10 @@
             dma((2, 4)), dma((2, 4)),
             dma((2,)), dma((2,)),
             dma((N_B - 1,)), dma((N_B,)),
+            dma((3,)),
         ],
         compiler_params=pltpu.CompilerParams(
-            collective_id=0, has_side_effects=True, vmem_limit_bytes=50 * 1024 * 1024
+            collective_id=0, has_side_effects=True, vmem_limit_bytes=VMEM
         ),
     )(
         cycle_points, legendre, coefficients.reshape(BLOCK, 2, 4, NT), spectra, sea_mask, wind_column,
@@ -624,9 +648,15 @@
     return pl.pallas_call(
         last,
         out_shape=(winds, waves, jax.ShapeDtypeStruct((CYCLES, SLOTS), F32)),
-        in_specs=[smem, vmem, vmem, vmem, vmem],
+        in_specs=[hbm, hbm, hbm, vmem, vmem],
         out_specs=(hbm, hbm, vmem),
-        scratch_shapes=[dma((2,))],
+        scratch_shapes=[
+            pltpu.SMEM((32,), jnp.int32),
+            pltpu.VMEM((1, CYCLES, 64, SLOTS), BF16),
+            pltpu.VMEM((ROWS, COLS, HALF), F32),
+            dma((6,)), dma((5,)),
+        ],
+        compiler_params=pltpu.CompilerParams(vmem_limit_bytes=VMEM),
     )(cycle_points, winds_done, waves_done, rough, roughness_source)
 
 

time: 54.4 us -> 47.1 us (0.87)
  local copies, waits for them, and re-layouts: 6.82 us -> 0 us
    unnamed x16 -> x0, local copies, waits for them, and re-layouts: 6.82 us -> none
    pallas_call x1, Pallas kernels: 43.4 us -> 42.6 us  [per_device(): pl.pallas_call(kernel, out_shape=(winds, waves, jax.ShapeDtypeStruct((N_B...]
where the time goes in v3:
time: 47.1 us; the launch traced here: 46.9 us
  Pallas kernels  46.3 us (98%)
  between operations  0.64 us (1%)
    pallas_call x1, Pallas kernels, per_device(): pl.pallas_call(kernel, out_shape=(winds, waves, jax.ShapeDtypeStruct((N_B...  42.6 us
    pallas_call x1, Pallas kernels, per_device(): pl.pallas_call(last, out_shape=(winds, waves, jax.ShapeDtypeStruct((CYCLE...  3.7 us

profile of v3, /device:TPU:1, one launch (start us, length us, event | category | flops | bytes accessed | tf_op | source)
XLA Modules:
  0.0 46.9 jit_solution(13219863314640910426)
XLA Ops:
  0.6 42.6 %shard_map.103 = (bf16[1,4,64,256]{3,2,1,0:T(8,128)(2,1)}, f32[16,32,648]{2,1,0:T(8,128)}, f32[16,8,128]{2,1,0:T(8,128)}) custom-call(s32[32]{0:T(128)} %cp_hbm.3, bf16[80,32,1280]{2,1,0:T(8,128)(2,1)} %leg_hbm.1, bf16[80,2,4,1280]{3,2,1,0:T(4,128)(2,1)} %bitcast.1, f32[16,32,648]{2,1,0:T(8,128)} %spec_hbm.1, s32[16,32]{1,0:T(8,128)} %mask_hbm.1, ...), custom_call_target="tpu_custom_call" | custom-call | tf_op jit(solution)/shard_map/pallas_call | solution.py:591
  43.2 3.7 %shard_map.104 = (bf16[1,4,64,256]{3,2,1,0:T(8,128)(2,1)}, f32[16,32,648]{2,1,0:T(8,128)}, f32[4,256]{1,0:T(4,128)}) custom-call(s32[32]{0:T(128)} %cp_hbm.3, bf16[1,4,64,256]{3,2,1,0:T(8,128)(2,1)} %get-tuple-element.6.gw_in, f32[16,32,648]{2,1,0:T(8,128)} %get-tuple-element.7.ws_in, f32[16,8,128]{2,1,0:T(8,128)} %get-tuple-element.8.rough, s32[4,256]{1,0:T(4,128)} %rs_ref.1), custom_call_target="tpu_custom_call" | custom-call | tf_op jit(solution)/shard_map/pallas_call | solution.py:648

commit v4 on v3

--- a/solution.py
+++ b/solution.py
@@ -114,7 +114,7 @@
     gw_out, ws_out, rough_out,
     gw_ref, ws_ref, rough, cp_ref, leg, coef, spec, mask_in, wc, cst_ref, sall, msg, a2a, a2x, gath, gperm, low_f, l0,
     table, ptable, ca, sa, buf_a, buf_b, d2, edge, edge_in,
-    mask_b, east_b, north_b, part, part_in, st, st_in,
+    mask_b, east_b, north_b, part, part_in, stress, order_in, order_out,
     i_sem, leg_sem, a_send, a_recv, x_send, x_recv, g_send, g_recv, l_send, l_recv, h_send, h_recv,
     c_send, c_recv, r_send, r_recv, o_sem,
 ):
@@ -147,6 +147,11 @@
         pl.semaphore_signal(barrier, inc=1, device_id={"aa": lax.rem(a + d, N_A)}, device_id_type=MESH)
     for d in range(1, N_B):
         pl.semaphore_signal(barrier, inc=1, device_id={"ba": lax.rem(b + d, N_B)}, device_id_type=MESH)
+
+    for d in range(1, N_B):
+        pl.semaphore_signal(
+            barrier, inc=1, device_id={"comp": 1 - s, "ba": lax.rem(b + d, N_B)}, device_id_type=MESH
+        )
 
     @pl.when(b == 0)
     def _():
@@ -193,7 +198,7 @@
                 acc = jnp.where(at, turned[key], acc)
             msg[t, :, q * 128 : q * 128 + 128] = acc
 
-    pl.semaphore_wait(barrier, N_A + N_B - 1 + jnp.where(b == 0, N_A - 1, 0))
+    pl.semaphore_wait(barrier, N_A + 2 * N_B - 2 + jnp.where(b == 0, N_A - 1, 0))
 
     sent = []
     for d in range(1, N_A):
@@ -310,11 +315,40 @@
     for l in range(CYCLES):
         tables(ptable, l, jnp.sum(side[l * 4 : l * 4 + 4, :], axis=0, keepdims=True), 2.0)
 
+    slots = lanes(1, SLOTS) + b * SLOTS
+    for l in range(CYCLES):
+        active = jnp.where(slots < cp_ref[a * CYCLES + l], 2.0, 0.0)
+        tables(table, l, slots.astype(F32), active)
+
     i, o = sublanes(384, 512), lanes(384, 512)
-    order = one_hot((o == (i & 3) * 128 + i // 4) & (i < BLOCK * 4))
+    order_in[...] = one_hot((o == (i & 3) * 128 + i // 4) & (i < BLOCK * 4))
+    r = sublanes(256, 256)
+    order_out[...] = one_hot(lanes(256, 256) == (r & 63) // 4 * 16 + r // 64 * 4 + (r & 3))
+
+    def upwind(buf, r, j, w):
+        c = lambda i: cst_ref[s, i : i + 1, j : j + w]
+        here = buf[r + 1, 8 : 8 + COLS, j : j + w]
+        ux = jnp.where(c(SE) > 0.0, buf[r + 1, 7 : 7 + COLS, j : j + w], buf[r + 1, 9 : 9 + COLS, j : j + w])
+        uy = jnp.where(c(SN) > 0.0, buf[r, 8 : 8 + COLS, j : j + w], buf[r + 2, 8 : 8 + COLS, j : j + w])
+        return here * c(CC) + ux * c(AE) + uy * c(AN)
+
+    halo_land(halo_a, buf_a, 0)
+
+    def second(r, carry):
+        m = mask_b[pl.ds(r * COLS, COLS), :]
+        for j, w in TILES:
+            v = upwind(buf_a, r, j, w) * m[:, :w]
+            buf_b[r + 1, 8 : 8 + COLS, j : j + w] = v
+            edge[1, 0, r, :, j : j + w] = v[0:1, :]
+            edge[1, 1, r, :, j : j + w] = v[COLS - 1 : COLS, :]
+        return carry
+
+    lax.fori_loop(0, ROWS, second, 0)
+    halo_b = halo(buf_b, 1)
+    halo_start(halo_b)
 
     def compact(landed):
-        wide = dot(landed[...].reshape(64, 384).astype(BF16), order)
+        wide = dot(landed[...].reshape(64, 384).astype(BF16), order_in[...])
         out = []
         for l in range(CYCLES):
             tiles = [jnp.zeros((8, 128), F32) for _ in range(WAVES // 128)]
@@ -385,34 +419,6 @@
     for t in x_peers:
         give(b, t)
 
-    def upwind(buf, r, j, w):
-        c = lambda i: cst_ref[s, i : i + 1, j : j + w]
-        here = buf[r + 1, 8 : 8 + COLS, j : j + w]
-        ux = jnp.where(c(SE) > 0.0, buf[r + 1, 7 : 7 + COLS, j : j + w], buf[r + 1, 9 : 9 + COLS, j : j + w])
-        uy = jnp.where(c(SN) > 0.0, buf[r, 8 : 8 + COLS, j : j + w], buf[r + 2, 8 : 8 + COLS, j : j + w])
-        return here * c(CC) + ux * c(AE) + uy * c(AN)
-
-    halo_land(halo_a, buf_a, 0)
-
-    def second(r, carry):
-        m = mask_b[pl.ds(r * COLS, COLS), :]
-        for j, w in TILES:
-            v = upwind(buf_a, r, j, w) * m[:, :w]
-            buf_b[r + 1, 8 : 8 + COLS, j : j + w] = v
-            edge[1, 0, r, :, j : j + w] = v[0:1, :]
-            edge[1, 1, r, :, j : j + w] = v[COLS - 1 : COLS, :]
-        return carry
-
-    lax.fori_loop(0, ROWS, second, 0)
-    halo_b = halo(buf_b, 1)
-    halo_start(halo_b)
-
-    for d in range(1, N_Z):
-        o = x * N_Z + lax.rem(z + N_Z - d, N_Z)
-        arrived(o)
-        for t in x_peers:
-            give(o, t)
-
     halo_land(halo_b, buf_b, 1)
 
     def third(r, carry):
@@ -434,6 +440,12 @@
     energy_copy = rcopy(part.at[0], part_in, c_send.at[0], c_recv.at[0], partner)
     energy_copy.start()
 
+    for d in range(1, N_Z):
+        o = x * N_Z + lax.rem(z + N_Z - d, N_Z)
+        arrived(o)
+        for t in x_peers:
+            give(o, t)
+
     @pl.when(b > 0)
     def _():
         low[0].wait_recv()
@@ -475,10 +487,16 @@
         total = jnp.sum(part[1, pl.ds(l * POINTS, POINTS), :], axis=1, keepdims=True)
         kept = jnp.where(sublanes(POINTS) == lanes(POINTS), jnp.broadcast_to(total, (POINTS, 128)), 0.0)
         row = jnp.sum(kept, axis=0, keepdims=True)
-        st[l : l + 1, :] = row
-        st[4 + l : 5 + l, :] = row
-    stress_copy = rcopy(st, st_in, c_send.at[1], c_recv.at[1], partner)
-    stress_copy.start()
+        stress[s, b, l : l + 1, :] = row
+        stress[s, b, 4 + l : 5 + l, :] = 0.12 * (east[l] * east[l] + north[l] * north[l]) + 0.02
+    band = [(s, lax.rem(b + d, N_B)) for d in range(1, N_B)] + [(1 - s, lax.rem(b + d, N_B)) for d in range(N_B)]
+    rough_copies = []
+    for n, (c, t) in enumerate(band):
+        own_block = stress.at[s, b]
+        rough_copies.append(
+            rcopy(own_block, own_block, r_send.at[n], r_recv.at[s, b], {"comp": c, "ba": t})
+        )
+        rough_copies[-1].start()
 
     energy_copy.wait_recv()
     for l in range(CYCLES):
@@ -500,39 +518,25 @@
     ws_copy = pltpu.make_async_copy(ws_ref, ws_out, o_sem.at[0])
     ws_copy.start()
 
-    stress_copy.wait_recv()
-    e, n = jnp.concatenate(east * 2, axis=0), jnp.concatenate(north * 2, axis=0)
-    air = 0.12 * (e * e + n * n) + 0.02
-    rough[b] = jnp.sqrt(1.0 + 0.03 * (st[...] + st_in[...]) / air)
-    rough_copies = []
-    for d in range(1, N_B):
-        t = lax.rem(b + d, N_B)
-        c = rcopy(rough.at[b], rough.at[b], r_send.at[d - 1], r_recv.at[b], {"ba": t})
-        c.start()
-        rough_copies.append(c)
-
-    slots = lanes(1, SLOTS) + b * SLOTS
-    for l in range(CYCLES):
-        active = jnp.where(slots < cp_ref[a * CYCLES + l], 2.0, 0.0)
-        tables(table, l, slots.astype(F32), active)
     for xd in range(1, N_X):
         for zd in range(N_Z):
             arrived(lax.rem(x + N_X - xd, N_X) * N_Z + lax.rem(z + zd, N_Z))
-    r = sublanes(256, 256)
-    order = one_hot(lanes(256, 256) == (r & 63) // 4 * 16 + r // 64 * 4 + (r & 3))
     for k in range(0, 2 * WAVES, 256):
-        gperm[:, k : k + 256] = dot(order, gath[:, :, k : k + 256].reshape(256, 256)).astype(BF16)
+        gperm[:, k : k + 256] = dot(order_out[...], gath[:, :, k : k + 256].reshape(256, 256)).astype(BF16)
     for l in range(CYCLES):
         gw_ref[0, l] = dot(gperm[l * 64 : l * 64 + 64, :], table[l]).astype(BF16)
     gw_copy = pltpu.make_async_copy(gw_ref, gw_out, o_sem.at[1])
     gw_copy.start()
 
-    for d in range(1, N_B):
-        o = lax.rem(b + N_B - d, N_B)
-        rcopy(rough.at[o], rough.at[o], r_send.at[0], r_recv.at[o], {"ba": o}).wait_recv()
+    for n, (c, t) in enumerate(band):
+        o = lax.rem(2 * b + N_B - t, N_B)
+        rcopy(stress.at[c, o], stress.at[c, o], r_send.at[n], r_recv.at[c, o], {"comp": c, "ba": o}).wait_recv()
+    total = stress[0, :, 0:4, :] + stress[1, :, 0:4, :]
+    rough[:, 0:4, :] = jnp.sqrt(1.0 + 0.03 * total / stress[0, :, 4:8, :])
+    rough[:, 4:8, :] = jnp.zeros((N_B, 4, 128), F32)
     rough_copy = pltpu.make_async_copy(rough, rough_out, o_sem.at[2])
     rough_copy.start()
-    for c in sent + gathers + rough_copies + [energy_copy, stress_copy]:
+    for c in sent + gathers + rough_copies + [energy_copy]:
         c.wait_send()
     halo_sent(halo_a)
     halo_sent(halo_b)
@@ -546,23 +550,29 @@
         c.wait()
 
 
-def last(cp_hbm, gw_in, ws_in, rough, rs_ref, gw_ref, ws_ref, ch_ref, cp_ref, gw, ws, sem_in, sem_out):
+def last(
+    cp_hbm, gw_in, ws_in, rough_in, rs_hbm, gw_ref, ws_ref, ch_ref, cp_ref, gw, ws, rough, rs_ref, sem_in, sem_out
+):
     a = lax.axis_index("aa")
     slots = lanes(1, SLOTS) + lax.axis_index("ba") * SLOTS
     step = ROWS // 4
     blocks = [pl.ds(i * step, step) for i in range(4)]
-    counts = pltpu.make_async_copy(cp_hbm, cp_ref, sem_in.at[5])
     come = [pltpu.make_async_copy(ws_in.at[k], ws.at[k], sem_in.at[i]) for i, k in enumerate(blocks)]
     come.append(pltpu.make_async_copy(gw_in, gw, sem_in.at[4]))
     go = [pltpu.make_async_copy(ws.at[k], ws_ref.at[k], sem_out.at[i]) for i, k in enumerate(blocks)]
     go.append(pltpu.make_async_copy(gw, gw_ref, sem_out.at[4]))
-    counts.start()
-    for c in come:
+    other = [
+        pltpu.make_async_copy(rough_in, rough, sem_in.at[5]),
+        pltpu.make_async_copy(rs_hbm, rs_ref, sem_in.at[6]),
+        pltpu.make_async_copy(cp_hbm, cp_ref, sem_in.at[7]),
+    ]
+    for c in other + come:
         c.start()
     for c, d in zip(come, go):
         c.wait()
         d.start()
-    counts.wait()
+    for c in other:
+        c.wait()
     for l in range(CYCLES):
         source = rs_ref[l : l + 1, :]
         low_part = ((source >> 9) & 3) * 32 + (source & 31)
@@ -626,16 +636,17 @@
             pltpu.VMEM((ROWS * COLS, 128), F32),
             pltpu.VMEM((2, ROWS * COLS, 128), F32),
             pltpu.VMEM((ROWS * COLS, 128), F32),
-            pltpu.VMEM((8, 128), F32),
-            pltpu.VMEM((8, 128), F32),
+            pltpu.VMEM((2, N_B, 8, 128), F32),
+            pltpu.VMEM((384, 512), BF16),
+            pltpu.VMEM((256, 256), BF16),
             dma((6,)), dma((GROUPS,)),
             dma((N_A - 1,)), dma((N_A,)),
             dma((N_A,)), dma((N_A,)),
             dma((N_B - 1,)), dma((N_B,)),
             dma((N_B - 1,)), dma((1,)),
             dma((2, 4)), dma((2, 4)),
-            dma((2,)), dma((2,)),
-            dma((N_B - 1,)), dma((N_B,)),
+            dma((1,)), dma((1,)),
+            dma((2 * N_B - 1,)), dma((2, N_B)),
             dma((3,)),
         ],
         compiler_params=pltpu.CompilerParams(
@@ -648,13 +659,15 @@
     return pl.pallas_call(
         last,
         out_shape=(winds, waves, jax.ShapeDtypeStruct((CYCLES, SLOTS), F32)),
-        in_specs=[hbm, hbm, hbm, vmem, vmem],
+        in_specs=[hbm] * 5,
         out_specs=(hbm, hbm, vmem),
         scratch_shapes=[
             pltpu.SMEM((32,), jnp.int32),
             pltpu.VMEM((1, CYCLES, 64, SLOTS), BF16),
             pltpu.VMEM((ROWS, COLS, HALF), F32),
-            dma((6,)), dma((5,)),
+            pltpu.VMEM((N_B, 8, 128), F32),
+            pltpu.VMEM((CYCLES, SLOTS), jnp.int32),
+            dma((8,)), dma((5,)),
         ],
         compiler_params=pltpu.CompilerParams(vmem_limit_bytes=VMEM),
     )(cycle_points, winds_done, waves_done, rough, roughness_source)

time: 47.1 us -> 48 us (1.019)
  the two profiles are of different devices: /device:TPU:1 before, /device:TPU:24 now
where the time goes in v4:
time: 48 us; the launch traced here: 47.9 us
  Pallas kernels  47.3 us (99%)
  between operations  0.64 us (1%)
    pallas_call x1, Pallas kernels, per_device(): pl.pallas_call(kernel, out_shape=(winds, waves, jax.ShapeDtypeStruct((N_B...  44.4 us
    pallas_call x1, Pallas kernels, per_device(): pl.pallas_call(last, out_shape=(winds, waves, jax.ShapeDtypeStruct((CYCLE...  2.93 us

profile of v4, /device:TPU:24, one launch (start us, length us, event | category | flops | bytes accessed | tf_op | source)
XLA Modules:
  0.0 47.9 jit_solution(13214913620139020037)
XLA Ops:
  0.6 44.4 %shard_map.103 = (bf16[1,4,64,256]{3,2,1,0:T(8,128)(2,1)}, f32[16,32,648]{2,1,0:T(8,128)}, f32[16,8,128]{2,1,0:T(8,128)}) custom-call(s32[32]{0:T(128)} %cp_hbm.3, bf16[80,32,1280]{2,1,0:T(8,128)(2,1)} %leg_hbm.1, bf16[80,2,4,1280]{3,2,1,0:T(4,128)(2,1)} %bitcast.1, f32[16,32,648]{2,1,0:T(8,128)} %spec_hbm.1, s32[16,32]{1,0:T(8,128)} %mask_hbm.1, ...), custom_call_target="tpu_custom_call" | custom-call | tf_op jit(solution)/shard_map/pallas_call | solution.py:601
  45.0 2.9 %shard_map.104 = (bf16[1,4,64,256]{3,2,1,0:T(8,128)(2,1)}, f32[16,32,648]{2,1,0:T(8,128)}, f32[4,256]{1,0:T(4,128)}) custom-call(s32[32]{0:T(128)} %cp_hbm.3, bf16[1,4,64,256]{3,2,1,0:T(8,128)(2,1)} %get-tuple-element.6.gw_in, f32[16,32,648]{2,1,0:T(8,128)} %get-tuple-element.7.ws_in, f32[16,8,128]{2,1,0:T(8,128)} %get-tuple-element.8.rough_in, s32[4,256]{1,0:T(4,128)} %rs_hbm.1), custom_call_target="tpu_custom_call" | custom-call | tf_op jit(solution)/shard_map/pallas_call | solution.py:659

commit v5 on v4

--- a/solution.py
+++ b/solution.py
@@ -42,6 +42,7 @@
     east = 0.45 * ratio * np.cos(theta)
     north = 0.45 * ratio * np.sin(theta)
     q = 2 * np.pi * freq / 9.81
+    assert (north[:HALF] > 0).all() and (north[HALF:] < 0).all()
     width = 0.1 * freq * (2 * np.pi / NDIR)
     rows = [
         np.abs(east),
@@ -124,13 +125,6 @@
     x, z = b // N_Z, b % N_Z
     partner = {"comp": 1 - s}
 
-    coef_copy = pltpu.make_async_copy(coef_hbm, coef, i_sem.at[0])
-    coef_copy.start()
-    leg_copies = lambda g: pltpu.make_async_copy(
-        leg_hbm.at[pl.ds(g * 8, 8)], leg.at[pl.ds(g * 8, 8)], leg_sem.at[g]
-    )
-    for g in range(GROUPS):
-        leg_copies(g).start()
     small = [
         pltpu.make_async_copy(mask_hbm, mask_in, i_sem.at[1]),
         pltpu.make_async_copy(wc_hbm, wc, i_sem.at[2]),
@@ -140,7 +134,13 @@
     ]
     for c in small:
         c.start()
-
+    coef_copy = pltpu.make_async_copy(coef_hbm, coef, i_sem.at[0])
+    coef_copy.start()
+    leg_copies = lambda g: pltpu.make_async_copy(
+        leg_hbm.at[pl.ds(g * 8, 8)], leg.at[pl.ds(g * 8, 8)], leg_sem.at[g]
+    )
+    for g in range(GROUPS):
+        leg_copies(g).start()
     barrier = pltpu.get_barrier_semaphore()
     pl.semaphore_signal(barrier, inc=1, device_id=partner, device_id_type=MESH)
     for d in range(1, N_A):
@@ -159,6 +159,61 @@
             pl.semaphore_signal(
                 barrier, inc=1, device_id={"comp": 1 - s, "aa": lax.rem(a + d, N_A)}, device_id_type=MESH
             )
+
+    for c in small:
+        c.wait()
+    sea = mask_in[...].astype(F32)
+    for r in range(ROWS):
+        mask_b[r * COLS : (r + 1) * COLS, :] = spread(sea[r : r + 1, :], COLS)
+
+    def first(r, carry):
+        m = mask_b[pl.ds(r * COLS, COLS), :]
+        for j, w in TILES:
+            v = spec[r, :, j : j + w] * m[:, :w]
+            buf_a[r + 1, 8 : 8 + COLS, j : j + w] = v
+            edge[0, 0, r, :, j : j + w] = v[0:1, :]
+            edge[0, 1, r, :, j : j + w] = v[COLS - 1 : COLS, :]
+        return carry
+
+    lax.fori_loop(0, ROWS, first, 0)
+
+    def halo(buf, step):
+        up = jnp.where(s == 0, N_A - 2 - a, a - 1)
+        down = jnp.where(s == 0, a - 1, N_A - 2 - a)
+        return [
+            (up >= 0, down >= 0, rcopy(
+                buf.at[ROWS - (ROWS - 1) * s, pl.ds(8, COLS)], buf.at[(ROWS + 1) * s, pl.ds(8, COLS)],
+                h_send.at[step, 0], h_recv.at[step, 0], {"aa": lax.rem(a + 1 + (N_A - 2) * s, N_A)})),
+            (b < N_B - 1, b > 0, rcopy(
+                edge.at[step, 1], edge_in.at[step, 0],
+                h_send.at[step, 1], h_recv.at[step, 1], {"ba": lax.rem(b + 1, N_B)})),
+            (b > 0, b < N_B - 1, rcopy(
+                edge.at[step, 0], edge_in.at[step, 1],
+                h_send.at[step, 2], h_recv.at[step, 2], {"ba": lax.rem(b + N_B - 1, N_B)})),
+        ]
+
+    def halo_start(copies):
+        for can, _, c in copies:
+            pl.when(can)(c.start)
+
+    def halo_land(copies, buf, step):
+        for i, (_, comes, c) in enumerate(copies):
+            pl.when(comes)(c.wait_recv)
+
+            @pl.when(jnp.logical_not(comes))
+            def _():
+                if i == 0:
+                    buf[(ROWS + 1) * s, 8 : 8 + COLS, :] = jnp.zeros((COLS, HALF), F32)
+                else:
+                    edge_in[step, i - 1] = jnp.zeros((ROWS, 1, HALF), F32)
+
+        for r in range(ROWS):
+            buf[r + 1, 7:8, :] = edge_in[step, 0, r]
+            buf[r + 1, 8 + COLS : 9 + COLS, :] = edge_in[step, 1, r]
+
+    def halo_sent(copies):
+        for can, _, c in copies:
+            pl.when(can)(c.wait_send)
 
     coef_copy.wait()
 
@@ -180,7 +235,11 @@
             sall[at, t * 128 : t * 128 + 128] = kept
         return carry
 
-    lax.fori_loop(0, GROUPS, legendre, 0)
+    lax.fori_loop(0, GROUPS // 2, legendre, 0)
+    pl.semaphore_wait(barrier, N_A + 2 * N_B - 2 + jnp.where(b == 0, N_A - 1, 0))
+    halo_a = halo(buf_a, 0)
+    halo_start(halo_a)
+    lax.fori_loop(GROUPS // 2, GROUPS, legendre, 0)
 
     i, o = sublanes(256, 256), lanes(256, 256)
     moved = dot(sall[...].astype(BF16), one_hot(o == (i & 31) // 4 * 32 + (i // 32) * 4 + (i & 3)))
@@ -198,8 +257,6 @@
                 acc = jnp.where(at, turned[key], acc)
             msg[t, :, q * 128 : q * 128 + 128] = acc
 
-    pl.semaphore_wait(barrier, N_A + 2 * N_B - 2 + jnp.where(b == 0, N_A - 1, 0))
-
     sent = []
     for d in range(1, N_A):
         t = lax.rem(a + d, N_A)
@@ -220,64 +277,6 @@
 
     a2a[a] = msg[a]
 
-    for c in small:
-        c.wait()
-    sea = mask_in[...].astype(F32)
-    for r in range(ROWS):
-        mask_b[r * COLS : (r + 1) * COLS, :] = spread(sea[r : r + 1, :], COLS)
-
-    def first(r, carry):
-        m = mask_b[pl.ds(r * COLS, COLS), :]
-        for j, w in TILES:
-            v = spec[r, :, j : j + w] * m[:, :w]
-            buf_a[r + 1, 8 : 8 + COLS, j : j + w] = v
-            edge[0, 0, r, :, j : j + w] = v[0:1, :]
-            edge[0, 1, r, :, j : j + w] = v[COLS - 1 : COLS, :]
-        return carry
-
-    lax.fori_loop(0, ROWS, first, 0)
-
-    def halo(buf, step):
-        return [
-            (a < N_A - 1, a > 0, rcopy(
-                buf.at[ROWS, pl.ds(8, COLS)], buf.at[0, pl.ds(8, COLS)],
-                h_send.at[step, 0], h_recv.at[step, 0], {"aa": lax.rem(a + 1, N_A)})),
-            (a > 0, a < N_A - 1, rcopy(
-                buf.at[1, pl.ds(8, COLS)], buf.at[ROWS + 1, pl.ds(8, COLS)],
-                h_send.at[step, 1], h_recv.at[step, 1], {"aa": lax.rem(a + N_A - 1, N_A)})),
-            (b < N_B - 1, b > 0, rcopy(
-                edge.at[step, 1], edge_in.at[step, 0],
-                h_send.at[step, 2], h_recv.at[step, 2], {"ba": lax.rem(b + 1, N_B)})),
-            (b > 0, b < N_B - 1, rcopy(
-                edge.at[step, 0], edge_in.at[step, 1],
-                h_send.at[step, 3], h_recv.at[step, 3], {"ba": lax.rem(b + N_B - 1, N_B)})),
-        ]
-
-    def halo_start(copies):
-        for can, _, c in copies:
-            pl.when(can)(c.start)
-
-    def halo_land(copies, buf, step):
-        for i, (_, comes, c) in enumerate(copies):
-            pl.when(comes)(c.wait_recv)
-
-            @pl.when(jnp.logical_not(comes))
-            def _():
-                if i < 2:
-                    buf[0 if i == 0 else ROWS + 1, 8 : 8 + COLS, :] = jnp.zeros((COLS, HALF), F32)
-                else:
-                    edge_in[step, i - 2] = jnp.zeros((ROWS, 1, HALF), F32)
-
-        for r in range(ROWS):
-            buf[r + 1, 7:8, :] = edge_in[step, 0, r]
-            buf[r + 1, 8 + COLS : 9 + COLS, :] = edge_in[step, 1, r]
-
-    def halo_sent(copies):
-        for can, _, c in copies:
-            pl.when(can)(c.wait_send)
-
-    halo_a = halo(buf_a, 0)
-    halo_start(halo_a)
 
     def tables(out, l, k, active):
         w = k.shape[1]
@@ -329,7 +328,7 @@
         c = lambda i: cst_ref[s, i : i + 1, j : j + w]
         here = buf[r + 1, 8 : 8 + COLS, j : j + w]
         ux = jnp.where(c(SE) > 0.0, buf[r + 1, 7 : 7 + COLS, j : j + w], buf[r + 1, 9 : 9 + COLS, j : j + w])
-        uy = jnp.where(c(SN) > 0.0, buf[r, 8 : 8 + COLS, j : j + w], buf[r + 2, 8 : 8 + COLS, j : j + w])
+        uy = buf[r + 2 * s, 8 : 8 + COLS, j : j + w]
         return here * c(CC) + ux * c(AE) + uy * c(AN)
 
     halo_land(halo_a, buf_a, 0)
@@ -644,7 +643,7 @@
             dma((N_A,)), dma((N_A,)),
             dma((N_B - 1,)), dma((N_B,)),
             dma((N_B - 1,)), dma((1,)),
-            dma((2, 4)), dma((2, 4)),
+            dma((2, 3)), dma((2, 3)),
             dma((1,)), dma((1,)),
             dma((2 * N_B - 1,)), dma((2, N_B)),
             dma((3,)),

time: 48 us -> 44.4 us (0.925)
  the two profiles are of different devices: /device:TPU:24 before, /device:TPU:1 now
where the time goes in v5:
time: 44.4 us; the launch traced here: 44.3 us
  Pallas kernels  43.7 us (98%)
  between operations  0.64 us (1%)
    pallas_call x1, Pallas kernels, per_device(): pl.pallas_call(kernel, out_shape=(winds, waves, jax.ShapeDtypeStruct((N_B...  40.8 us
    pallas_call x1, Pallas kernels, per_device(): pl.pallas_call(last, out_shape=(winds, waves, jax.ShapeDtypeStruct((CYCLE...  2.93 us

profile of v5, /device:TPU:1, one launch (start us, length us, event | category | flops | bytes accessed | tf_op | source)
XLA Modules:
  0.0 44.3 jit_solution(17595854613875000420)
XLA Ops:
  0.6 40.8 %shard_map.103 = (bf16[1,4,64,256]{3,2,1,0:T(8,128)(2,1)}, f32[16,32,648]{2,1,0:T(8,128)}, f32[16,8,128]{2,1,0:T(8,128)}) custom-call(s32[32]{0:T(128)} %cp_hbm.3, bf16[80,32,1280]{2,1,0:T(8,128)(2,1)} %leg_hbm.1, bf16[80,2,4,1280]{3,2,1,0:T(4,128)(2,1)} %bitcast.1, f32[16,32,648]{2,1,0:T(8,128)} %spec_hbm.1, s32[16,32]{1,0:T(8,128)} %mask_hbm.1, ...), custom_call_target="tpu_custom_call" | custom-call | tf_op jit(solution)/shard_map/pallas_call | solution.py:600
  41.4 2.9 %shard_map.104 = (bf16[1,4,64,256]{3,2,1,0:T(8,128)(2,1)}, f32[16,32,648]{2,1,0:T(8,128)}, f32[4,256]{1,0:T(4,128)}) custom-call(s32[32]{0:T(128)} %cp_hbm.3, bf16[1,4,64,256]{3,2,1,0:T(8,128)(2,1)} %get-tuple-element.6.gw_in, f32[16,32,648]{2,1,0:T(8,128)} %get-tuple-element.7.ws_in, f32[16,8,128]{2,1,0:T(8,128)} %get-tuple-element.8.rough_in, s32[4,256]{1,0:T(4,128)} %rs_hbm.1), custom_call_target="tpu_custom_call" | custom-call | tf_op jit(solution)/shard_map/pallas_call | solution.py:658

commit v6 on v5

--- a/solution.py
+++ b/solution.py
@@ -31,6 +31,7 @@
 VMEM = 64_000_000
 HALF = NDIR * NFREQ // 2
 POINTS = 128
+FAR = [(2, 3), (2, 2), (1, 3), (3, 3), (2, 1), (1, 2), (3, 2), (0, 3), (1, 1), (3, 1), (2, 0), (0, 2), (1, 0), (3, 0), (0, 1)]
 TILES = [(j, min(128, HALF - j)) for j in range(0, HALF, 128)]
 
 
@@ -114,7 +115,7 @@
     cp_hbm, leg_hbm, coef_hbm, spec_hbm, mask_hbm, wc_hbm, cst_hbm,
     gw_out, ws_out, rough_out,
     gw_ref, ws_ref, rough, cp_ref, leg, coef, spec, mask_in, wc, cst_ref, sall, msg, a2a, a2x, gath, gperm, low_f, l0,
-    table, ptable, ca, sa, buf_a, buf_b, d2, edge, edge_in,
+    table, ptable, ca, sa, buf_a, buf_b, d2, edge, edge_in, row_out, row_in,
     mask_b, east_b, north_b, part, part_in, stress, order_in, order_out,
     i_sem, leg_sem, a_send, a_recv, x_send, x_recv, g_send, g_recv, l_send, l_recv, h_send, h_recv,
     c_send, c_recv, r_send, r_recv, o_sem,
@@ -125,6 +126,12 @@
     x, z = b // N_Z, b % N_Z
     partner = {"comp": 1 - s}
 
+    flips = lambda v: {0: v, 1: v + 1 - 2 * (v % 2), 2: lax.rem(v + 2, 4), 3: 3 - v}
+    flip_x, flip_z, flip_y = flips(x), flips(z), flips(a % 4)
+    half = a // 4
+    peers_a = [(1 - half) * 4 + flip_y[i] for i in (2, 1, 3, 0)] + [half * 4 + flip_y[i] for i in (2, 1, 3)]
+    peers_b = [flip_x[i] * N_Z + flip_z[j] for i, j in FAR]
+
     small = [
         pltpu.make_async_copy(mask_hbm, mask_in, i_sem.at[1]),
         pltpu.make_async_copy(wc_hbm, wc, i_sem.at[2]),
@@ -132,8 +139,6 @@
         pltpu.make_async_copy(spec_hbm, spec, i_sem.at[4]),
         pltpu.make_async_copy(cp_hbm, cp_ref, i_sem.at[5]),
     ]
-    for c in small:
-        c.start()
     coef_copy = pltpu.make_async_copy(coef_hbm, coef, i_sem.at[0])
     coef_copy.start()
     leg_copies = lambda g: pltpu.make_async_copy(
@@ -141,48 +146,27 @@
     )
     for g in range(GROUPS):
         leg_copies(g).start()
+    for c in small:
+        c.start()
     barrier = pltpu.get_barrier_semaphore()
     pl.semaphore_signal(barrier, inc=1, device_id=partner, device_id_type=MESH)
-    for d in range(1, N_A):
-        pl.semaphore_signal(barrier, inc=1, device_id={"aa": lax.rem(a + d, N_A)}, device_id_type=MESH)
-    for d in range(1, N_B):
-        pl.semaphore_signal(barrier, inc=1, device_id={"ba": lax.rem(b + d, N_B)}, device_id_type=MESH)
-
-    for d in range(1, N_B):
-        pl.semaphore_signal(
-            barrier, inc=1, device_id={"comp": 1 - s, "ba": lax.rem(b + d, N_B)}, device_id_type=MESH
-        )
+    for t in peers_a:
+        pl.semaphore_signal(barrier, inc=1, device_id={"aa": t}, device_id_type=MESH)
+    for t in peers_b:
+        pl.semaphore_signal(barrier, inc=1, device_id={"ba": t}, device_id_type=MESH)
+        pl.semaphore_signal(barrier, inc=1, device_id={"comp": 1 - s, "ba": t}, device_id_type=MESH)
 
     @pl.when(b == 0)
     def _():
-        for d in range(1, N_A):
-            pl.semaphore_signal(
-                barrier, inc=1, device_id={"comp": 1 - s, "aa": lax.rem(a + d, N_A)}, device_id_type=MESH
-            )
-
-    for c in small:
-        c.wait()
-    sea = mask_in[...].astype(F32)
-    for r in range(ROWS):
-        mask_b[r * COLS : (r + 1) * COLS, :] = spread(sea[r : r + 1, :], COLS)
-
-    def first(r, carry):
-        m = mask_b[pl.ds(r * COLS, COLS), :]
-        for j, w in TILES:
-            v = spec[r, :, j : j + w] * m[:, :w]
-            buf_a[r + 1, 8 : 8 + COLS, j : j + w] = v
-            edge[0, 0, r, :, j : j + w] = v[0:1, :]
-            edge[0, 1, r, :, j : j + w] = v[COLS - 1 : COLS, :]
-        return carry
-
-    lax.fori_loop(0, ROWS, first, 0)
+        for t in peers_a:
+            pl.semaphore_signal(barrier, inc=1, device_id={"comp": 1 - s, "aa": t}, device_id_type=MESH)
 
     def halo(buf, step):
         up = jnp.where(s == 0, N_A - 2 - a, a - 1)
         down = jnp.where(s == 0, a - 1, N_A - 2 - a)
         return [
             (up >= 0, down >= 0, rcopy(
-                buf.at[ROWS - (ROWS - 1) * s, pl.ds(8, COLS)], buf.at[(ROWS + 1) * s, pl.ds(8, COLS)],
+                row_out.at[step], row_in.at[step],
                 h_send.at[step, 0], h_recv.at[step, 0], {"aa": lax.rem(a + 1 + (N_A - 2) * s, N_A)})),
             (b < N_B - 1, b > 0, rcopy(
                 edge.at[step, 1], edge_in.at[step, 0],
@@ -192,7 +176,8 @@
                 h_send.at[step, 2], h_recv.at[step, 2], {"ba": lax.rem(b + N_B - 1, N_B)})),
         ]
 
-    def halo_start(copies):
+    def halo_start(copies, buf, step):
+        row_out[step] = buf[ROWS - (ROWS - 1) * s, 8 : 8 + COLS, :].astype(BF16)
         for can, _, c in copies:
             pl.when(can)(c.start)
 
@@ -203,10 +188,11 @@
             @pl.when(jnp.logical_not(comes))
             def _():
                 if i == 0:
-                    buf[(ROWS + 1) * s, 8 : 8 + COLS, :] = jnp.zeros((COLS, HALF), F32)
+                    row_in[step] = jnp.zeros((COLS, HALF), BF16)
                 else:
                     edge_in[step, i - 1] = jnp.zeros((ROWS, 1, HALF), F32)
 
+        buf[(ROWS + 1) * s, 8 : 8 + COLS, :] = row_in[step].astype(F32)
         for r in range(ROWS):
             buf[r + 1, 7:8, :] = edge_in[step, 0, r]
             buf[r + 1, 8 + COLS : 9 + COLS, :] = edge_in[step, 1, r]
@@ -235,11 +221,7 @@
             sall[at, t * 128 : t * 128 + 128] = kept
         return carry
 
-    lax.fori_loop(0, GROUPS // 2, legendre, 0)
-    pl.semaphore_wait(barrier, N_A + 2 * N_B - 2 + jnp.where(b == 0, N_A - 1, 0))
-    halo_a = halo(buf_a, 0)
-    halo_start(halo_a)
-    lax.fori_loop(GROUPS // 2, GROUPS, legendre, 0)
+    lax.fori_loop(0, GROUPS, legendre, 0)
 
     i, o = sublanes(256, 256), lanes(256, 256)
     moved = dot(sall[...].astype(BF16), one_hot(o == (i & 31) // 4 * 32 + (i // 32) * 4 + (i & 3)))
@@ -257,15 +239,14 @@
                 acc = jnp.where(at, turned[key], acc)
             msg[t, :, q * 128 : q * 128 + 128] = acc
 
+    pl.semaphore_wait(barrier, N_A + 2 * N_B - 2 + jnp.where(b == 0, N_A - 1, 0))
     sent = []
-    for d in range(1, N_A):
-        t = lax.rem(a + d, N_A)
-        c = rcopy(msg.at[t], a2a.at[a], a_send.at[d - 1], a_recv.at[a], {"aa": t})
+    for d, t in enumerate(peers_a):
+        c = rcopy(msg.at[t], a2a.at[a], a_send.at[d], a_recv.at[a], {"aa": t})
         c.start()
         sent.append(c)
     crossed = []
-    for d in range(N_A):
-        t = lax.rem(a + d, N_A)
+    for d, t in enumerate(peers_a + [a]):
         crossed.append(
             rcopy(msg.at[t], a2x.at[a], x_send.at[d], x_recv.at[a], {"comp": 1 - s, "aa": t})
         )
@@ -277,6 +258,26 @@
 
     a2a[a] = msg[a]
 
+
+    for c in small:
+        c.wait()
+    sea = mask_in[...].astype(F32)
+    for r in range(ROWS):
+        mask_b[r * COLS : (r + 1) * COLS, :] = spread(sea[r : r + 1, :], COLS)
+
+    def first(r, carry):
+        m = mask_b[pl.ds(r * COLS, COLS), :]
+        for j, w in TILES:
+            v = spec[r, :, j : j + w] * m[:, :w]
+            buf_a[r + 1, 8 : 8 + COLS, j : j + w] = v
+            edge[0, 0, r, :, j : j + w] = v[0:1, :]
+            edge[0, 1, r, :, j : j + w] = v[COLS - 1 : COLS, :]
+        return carry
+
+    lax.fori_loop(0, ROWS, first, 0)
+
+    halo_a = halo(buf_a, 0)
+    halo_start(halo_a, buf_a, 0)
 
     def tables(out, l, k, active):
         w = k.shape[1]
@@ -344,7 +345,7 @@
 
     lax.fori_loop(0, ROWS, second, 0)
     halo_b = halo(buf_b, 1)
-    halo_start(halo_b)
+    halo_start(halo_b, buf_b, 1)
 
     def compact(landed):
         wide = dot(landed[...].reshape(64, 384).astype(BF16), order_in[...])
@@ -371,19 +372,17 @@
                     r = base + p * 4 + l
                     low_f[r : r + 1, t * 128 : t * 128 + 128] = blocks[l][t][p * 4 : p * 4 + 1, :]
 
-    for d in range(1, N_A):
-        c = lax.rem(a + N_A - d, N_A)
-        rcopy(msg.at[0], a2a.at[c], a_send.at[d - 1], a_recv.at[c], {"aa": c}).wait_recv()
+    for d, c in enumerate(peers_a):
+        rcopy(msg.at[0], a2a.at[c], a_send.at[d], a_recv.at[c], {"aa": c}).wait_recv()
     blocks = compact(a2a)
     low = [
-        rcopy(l0, l0, l_send.at[d - 1], l_recv.at[0], {"ba": lax.rem(b + d, N_B)}) for d in range(1, N_B)
+        rcopy(l0, l0, l_send.at[d], l_recv.at[0], {"ba": t}) for d, t in enumerate(peers_b)
     ]
 
     @pl.when(b == 0)
     def _():
         lowest(blocks, 0)
-        for d in range(N_A):
-            c = lax.rem(a + N_A - d, N_A)
+        for d, c in enumerate(peers_a + [a]):
             rcopy(msg.at[0], a2x.at[c], x_send.at[d], x_recv.at[c], {"comp": 1 - s, "aa": c}).wait_recv()
         lowest(compact(a2x), 8)
         l0[...] = low_f[...].astype(BF16)
@@ -412,9 +411,9 @@
     def arrived(o):
         rcopy(gath.at[o], gath.at[o], g_send.at[0], g_recv.at[o], {"ba": o}).wait_recv()
 
-    x_peers = [lax.rem(x + d, N_X) * N_Z + z for d in (1, 3, 2)]
-    for d in range(1, N_Z):
-        give(b, x * N_Z + lax.rem(z + d, N_Z))
+    x_peers = [flip_x[i] * N_Z + z for i in (2, 1, 3)]
+    for i in (3, 2, 1):
+        give(b, x * N_Z + flip_z[i])
     for t in x_peers:
         give(b, t)
 
@@ -439,8 +438,8 @@
     energy_copy = rcopy(part.at[0], part_in, c_send.at[0], c_recv.at[0], partner)
     energy_copy.start()
 
-    for d in range(1, N_Z):
-        o = x * N_Z + lax.rem(z + N_Z - d, N_Z)
+    for i in (1, 2, 3):
+        o = x * N_Z + flip_z[i]
         arrived(o)
         for t in x_peers:
             give(o, t)
@@ -488,7 +487,7 @@
         row = jnp.sum(kept, axis=0, keepdims=True)
         stress[s, b, l : l + 1, :] = row
         stress[s, b, 4 + l : 5 + l, :] = 0.12 * (east[l] * east[l] + north[l] * north[l]) + 0.02
-    band = [(s, lax.rem(b + d, N_B)) for d in range(1, N_B)] + [(1 - s, lax.rem(b + d, N_B)) for d in range(N_B)]
+    band = [(c, t) for t in peers_b for c in (1 - s, s)] + [(1 - s, b)]
     rough_copies = []
     for n, (c, t) in enumerate(band):
         own_block = stress.at[s, b]
@@ -528,8 +527,7 @@
     gw_copy.start()
 
     for n, (c, t) in enumerate(band):
-        o = lax.rem(2 * b + N_B - t, N_B)
-        rcopy(stress.at[c, o], stress.at[c, o], r_send.at[n], r_recv.at[c, o], {"comp": c, "ba": o}).wait_recv()
+        rcopy(stress.at[c, t], stress.at[c, t], r_send.at[n], r_recv.at[c, t], {"comp": c, "ba": t}).wait_recv()
     total = stress[0, :, 0:4, :] + stress[1, :, 0:4, :]
     rough[:, 0:4, :] = jnp.sqrt(1.0 + 0.03 * total / stress[0, :, 4:8, :])
     rough[:, 4:8, :] = jnp.zeros((N_B, 4, 128), F32)
@@ -630,6 +628,8 @@
             pltpu.VMEM((ROWS, COLS, HALF), F32),
             pltpu.VMEM((2, 2, ROWS, 1, HALF), F32),
             pltpu.VMEM((2, 2, ROWS, 1, HALF), F32),
+            pltpu.VMEM((2, COLS, HALF), BF16),
+            pltpu.VMEM((2, COLS, HALF), BF16),
             pltpu.VMEM((ROWS * COLS, 128), F32),
             pltpu.VMEM((ROWS * COLS, 128), F32),
             pltpu.VMEM((ROWS * COLS, 128), F32),

time: 44.4 us -> 44 us (level); the launches traced: 44.3 us -> 43.1 us
  Pallas kernels: 43.7 us -> 42.5 us
    pallas_call x1, Pallas kernels: 40.8 us -> 39.6 us  [per_device(): pl.pallas_call(kernel, out_shape=(winds, waves, jax.ShapeDtypeStruct((N_B...]
where the time goes in v6:
time: 44 us; the launch traced here: 43.1 us
  Pallas kernels  42.5 us (97%)
  between operations  0.64 us (1%)
    pallas_call x1, Pallas kernels, per_device(): pl.pallas_call(kernel, out_shape=(winds, waves, jax.ShapeDtypeStruct((N_B...  39.6 us
    pallas_call x1, Pallas kernels, per_device(): pl.pallas_call(last, out_shape=(winds, waves, jax.ShapeDtypeStruct((CYCLE...  2.93 us

profile of v6, /device:TPU:1, one launch (start us, length us, event | category | flops | bytes accessed | tf_op | source)
XLA Modules:
  0.0 43.1 jit_solution(15826864723112234984)
XLA Ops:
  0.6 39.6 %shard_map.103 = (bf16[1,4,64,256]{3,2,1,0:T(8,128)(2,1)}, f32[16,32,648]{2,1,0:T(8,128)}, f32[16,8,128]{2,1,0:T(8,128)}) custom-call(s32[32]{0:T(128)} %cp_hbm.3, bf16[80,32,1280]{2,1,0:T(8,128)(2,1)} %leg_hbm.1, bf16[80,2,4,1280]{3,2,1,0:T(4,128)(2,1)} %bitcast.1, f32[16,32,648]{2,1,0:T(8,128)} %spec_hbm.1, s32[16,32]{1,0:T(8,128)} %mask_hbm.1, ...), custom_call_target="tpu_custom_call" | custom-call | tf_op jit(solution)/shard_map/pallas_call | solution.py:598
  40.2 2.9 %shard_map.104 = (bf16[1,4,64,256]{3,2,1,0:T(8,128)(2,1)}, f32[16,32,648]{2,1,0:T(8,128)}, f32[4,256]{1,0:T(4,128)}) custom-call(s32[32]{0:T(128)} %cp_hbm.3, bf16[1,4,64,256]{3,2,1,0:T(8,128)(2,1)} %get-tuple-element.6.gw_in, f32[16,32,648]{2,1,0:T(8,128)} %get-tuple-element.7.ws_in, f32[16,8,128]{2,1,0:T(8,128)} %get-tuple-element.8.rough_in, s32[4,256]{1,0:T(4,128)} %rs_hbm.1), custom_call_target="tpu_custom_call" | custom-call | tf_op jit(solution)/shard_map/pallas_call | solution.py:658

commit v7 on v6

--- a/solution.py
+++ b/solution.py
@@ -114,7 +114,7 @@
 def kernel(
     cp_hbm, leg_hbm, coef_hbm, spec_hbm, mask_hbm, wc_hbm, cst_hbm,
     gw_out, ws_out, rough_out,
-    gw_ref, ws_ref, rough, cp_ref, leg, coef, spec, mask_in, wc, cst_ref, sall, msg, a2a, a2x, gath, gperm, low_f, l0,
+    gw_ref, ws_ref, rough, cp_ref, leg, coef, degrees, spec, mask_in, wc, cst_ref, sall, msg, a2a, a2x, gath, gperm, low_f, l0,
     table, ptable, ca, sa, buf_a, buf_b, d2, edge, edge_in, row_out, row_in,
     mask_b, east_b, north_b, part, part_in, stress, order_in, order_out,
     i_sem, leg_sem, a_send, a_recv, x_send, x_recv, g_send, g_recv, l_send, l_recv, h_send, h_recv,
@@ -203,15 +203,20 @@
 
     coef_copy.wait()
 
-    def legendre(g, carry):
+    def masked(g, carry):
         rows = []
         for i in range(8):
             order = a * BLOCK + g * 8 + i
             block = jnp.concatenate([coef[g * 8 + i, p].astype(F32) for p in range(2)], axis=0)
             rows.append(jnp.where(lanes(8, NT) >= order, block, 0.0))
-        rows = jnp.concatenate(rows, axis=0).astype(BF16)
+        degrees[g] = jnp.concatenate(rows, axis=0).astype(BF16)
+        return carry
+
+    lax.fori_loop(0, GROUPS, masked, 0)
+
+    def legendre(g, carry):
         leg_copies(g).wait()
-        cross = dot(rows, leg[pl.ds(g * 8, 8)].reshape(256, NT), ((1,), (1,)))
+        cross = dot(degrees[g], leg[pl.ds(g * 8, 8)].reshape(256, NT), ((1,), (1,)))
         at = pl.ds(pl.multiple_of(g * 8, 8), 8)
         for t in range(2):
             kept = cross[t * 32 : t * 32 + 8, t * 128 : t * 128 + 128]
@@ -411,9 +416,9 @@
     def arrived(o):
         rcopy(gath.at[o], gath.at[o], g_send.at[0], g_recv.at[o], {"ba": o}).wait_recv()
 
-    x_peers = [flip_x[i] * N_Z + z for i in (2, 1, 3)]
-    for i in (3, 2, 1):
-        give(b, x * N_Z + flip_z[i])
+    x_peers = [lax.rem(x + d, N_X) * N_Z + z for d in (1, 3, 2)]
+    for d in range(1, N_Z):
+        give(b, x * N_Z + lax.rem(z + d, N_Z))
     for t in x_peers:
         give(b, t)
 
@@ -438,8 +443,8 @@
     energy_copy = rcopy(part.at[0], part_in, c_send.at[0], c_recv.at[0], partner)
     energy_copy.start()
 
-    for i in (1, 2, 3):
-        o = x * N_Z + flip_z[i]
+    for d in range(1, N_Z):
+        o = x * N_Z + lax.rem(z + N_Z - d, N_Z)
         arrived(o)
         for t in x_peers:
             give(o, t)
@@ -607,6 +612,7 @@
             pltpu.SMEM((32,), jnp.int32),
             pltpu.VMEM((BLOCK, 32, NT), BF16),
             pltpu.VMEM((BLOCK, 2, 4, NT), BF16),
+            pltpu.VMEM((GROUPS, 64, NT), BF16),
             pltpu.VMEM((ROWS, COLS, HALF), F32),
             pltpu.VMEM((ROWS, COLS), jnp.int32),
             pltpu.VMEM((ROWS, 512), jnp.int32),

time: 44 us -> 43.8 us (level); the launches traced: 43.1 us -> 43.7 us
  Pallas kernels: 42.5 us -> 43.1 us
    pallas_call x1, Pallas kernels: 39.6 us -> 40.2 us  [per_device(): pl.pallas_call(kernel, out_shape=(winds, waves, jax.ShapeDtypeStruct((N_B...]
where the time goes in v7:
time: 43.8 us; the launch traced here: 43.7 us
  Pallas kernels  43.1 us (98%)
  between operations  0.64 us (1%)
    pallas_call x1, Pallas kernels, per_device(): pl.pallas_call(kernel, out_shape=(winds, waves, jax.ShapeDtypeStruct((N_B...  40.2 us
    pallas_call x1, Pallas kernels, per_device(): pl.pallas_call(last, out_shape=(winds, waves, jax.ShapeDtypeStruct((CYCLE...  2.93 us

profile of v7, /device:TPU:1, one launch (start us, length us, event | category | flops | bytes accessed | tf_op | source)
XLA Modules:
  0.0 43.7 jit_solution(2380157984474706423)
XLA Ops:
  0.6 40.2 %shard_map.103 = (bf16[1,4,64,256]{3,2,1,0:T(8,128)(2,1)}, f32[16,32,648]{2,1,0:T(8,128)}, f32[16,8,128]{2,1,0:T(8,128)}) custom-call(s32[32]{0:T(128)} %cp_hbm.3, bf16[80,32,1280]{2,1,0:T(8,128)(2,1)} %leg_hbm.1, bf16[80,2,4,1280]{3,2,1,0:T(4,128)(2,1)} %bitcast.1, f32[16,32,648]{2,1,0:T(8,128)} %spec_hbm.1, s32[16,32]{1,0:T(8,128)} %mask_hbm.1, ...), custom_call_target="tpu_custom_call" | custom-call | tf_op jit(solution)/shard_map/pallas_call | solution.py:603
  40.8 2.9 %shard_map.104 = (bf16[1,4,64,256]{3,2,1,0:T(8,128)(2,1)}, f32[16,32,648]{2,1,0:T(8,128)}, f32[4,256]{1,0:T(4,128)}) custom-call(s32[32]{0:T(128)} %cp_hbm.3, bf16[1,4,64,256]{3,2,1,0:T(8,128)(2,1)} %get-tuple-element.6.gw_in, f32[16,32,648]{2,1,0:T(8,128)} %get-tuple-element.7.ws_in, f32[16,8,128]{2,1,0:T(8,128)} %get-tuple-element.8.rough_in, s32[4,256]{1,0:T(4,128)} %rs_hbm.1), custom_call_target="tpu_custom_call" | custom-call | tf_op jit(solution)/shard_map/pallas_call | solution.py:664

commit v8 on v7

--- a/solution.py
+++ b/solution.py
@@ -443,11 +443,16 @@
     energy_copy = rcopy(part.at[0], part_in, c_send.at[0], c_recv.at[0], partner)
     energy_copy.start()
 
-    for d in range(1, N_Z):
-        o = x * N_Z + lax.rem(z + N_Z - d, N_Z)
+    z_peers = [x * N_Z + lax.rem(z + d, N_Z) for d in range(1, N_Z)]
+    across = lax.rem(x + 2, N_X)
+    for n, o in enumerate(z_peers):
         arrived(o)
-        for t in x_peers:
+        for t in x_peers[:2]:
             give(o, t)
+        if n == 0:
+            arrived(across * N_Z + z)
+            for t in z_peers:
+                give(across * N_Z + z, t)
 
     @pl.when(b > 0)
     def _():
@@ -521,9 +526,10 @@
     ws_copy = pltpu.make_async_copy(ws_ref, ws_out, o_sem.at[0])
     ws_copy.start()
 
-    for xd in range(1, N_X):
+    for xd in (1, 3, 2):
         for zd in range(N_Z):
-            arrived(lax.rem(x + N_X - xd, N_X) * N_Z + lax.rem(z + zd, N_Z))
+            if (xd, zd) != (2, 0):
+                arrived(lax.rem(x + xd, N_X) * N_Z + lax.rem(z + zd, N_Z))
     for k in range(0, 2 * WAVES, 256):
         gperm[:, k : k + 256] = dot(order_out[...], gath[:, :, k : k + 256].reshape(256, 256)).astype(BF16)
     for l in range(CYCLES):

time: 43.8 us -> 45.3 us (1.034)
  Pallas kernels: 43.1 us -> 44.5 us
    pallas_call x1, Pallas kernels: 40.2 us -> 41.6 us  [per_device(): pl.pallas_call(kernel, out_shape=(winds, waves, jax.ShapeDtypeStruct((N_B...]
where the time goes in v8:
time: 45.3 us; the launch traced here: 45.2 us
  Pallas kernels  44.5 us (98%)
  between operations  0.64 us (1%)
    pallas_call x1, Pallas kernels, per_device(): pl.pallas_call(kernel, out_shape=(winds, waves, jax.ShapeDtypeStruct((N_B...  41.6 us
    pallas_call x1, Pallas kernels, per_device(): pl.pallas_call(last, out_shape=(winds, waves, jax.ShapeDtypeStruct((CYCLE...  2.93 us

profile of v8, /device:TPU:1, one launch (start us, length us, event | category | flops | bytes accessed | tf_op | source)
XLA Modules:
  0.0 45.2 jit_solution(15617255302187544002)
XLA Ops:
  0.6 41.6 %shard_map.103 = (bf16[1,4,64,256]{3,2,1,0:T(8,128)(2,1)}, f32[16,32,648]{2,1,0:T(8,128)}, f32[16,8,128]{2,1,0:T(8,128)}) custom-call(s32[32]{0:T(128)} %cp_hbm.3, bf16[80,32,1280]{2,1,0:T(8,128)(2,1)} %leg_hbm.1, bf16[80,2,4,1280]{3,2,1,0:T(4,128)(2,1)} %bitcast.1, f32[16,32,648]{2,1,0:T(8,128)} %spec_hbm.1, s32[16,32]{1,0:T(8,128)} %mask_hbm.1, ...), custom_call_target="tpu_custom_call" | custom-call | tf_op jit(solution)/shard_map/pallas_call | solution.py:609
  42.3 2.9 %shard_map.104 = (bf16[1,4,64,256]{3,2,1,0:T(8,128)(2,1)}, f32[16,32,648]{2,1,0:T(8,128)}, f32[4,256]{1,0:T(4,128)}) custom-call(s32[32]{0:T(128)} %cp_hbm.3, bf16[1,4,64,256]{3,2,1,0:T(8,128)(2,1)} %get-tuple-element.6.gw_in, f32[16,32,648]{2,1,0:T(8,128)} %get-tuple-element.7.ws_in, f32[16,8,128]{2,1,0:T(8,128)} %get-tuple-element.8.rough_in, s32[4,256]{1,0:T(4,128)} %rs_hbm.1), custom_call_target="tpu_custom_call" | custom-call | tf_op jit(solution)/shard_map/pallas_call | solution.py:670

commit v9 on v7

--- a/solution.py
+++ b/solution.py
@@ -116,7 +116,7 @@
     gw_out, ws_out, rough_out,
     gw_ref, ws_ref, rough, cp_ref, leg, coef, degrees, spec, mask_in, wc, cst_ref, sall, msg, a2a, a2x, gath, gperm, low_f, l0,
     table, ptable, ca, sa, buf_a, buf_b, d2, edge, edge_in, row_out, row_in,
-    mask_b, east_b, north_b, part, part_in, stress, order_in, order_out,
+    mask_b, east_b, north_b, part, part_in, st, st_in, order_in, order_out,
     i_sem, leg_sem, a_send, a_recv, x_send, x_recv, g_send, g_recv, l_send, l_recv, h_send, h_recv,
     c_send, c_recv, r_send, r_recv, o_sem,
 ):
@@ -154,7 +154,6 @@
         pl.semaphore_signal(barrier, inc=1, device_id={"aa": t}, device_id_type=MESH)
     for t in peers_b:
         pl.semaphore_signal(barrier, inc=1, device_id={"ba": t}, device_id_type=MESH)
-        pl.semaphore_signal(barrier, inc=1, device_id={"comp": 1 - s, "ba": t}, device_id_type=MESH)
 
     @pl.when(b == 0)
     def _():
@@ -244,7 +243,7 @@
                 acc = jnp.where(at, turned[key], acc)
             msg[t, :, q * 128 : q * 128 + 128] = acc
 
-    pl.semaphore_wait(barrier, N_A + 2 * N_B - 2 + jnp.where(b == 0, N_A - 1, 0))
+    pl.semaphore_wait(barrier, N_A + N_B - 1 + jnp.where(b == 0, N_A - 1, 0))
     sent = []
     for d, t in enumerate(peers_a):
         c = rcopy(msg.at[t], a2a.at[a], a_send.at[d], a_recv.at[a], {"aa": t})
@@ -327,8 +326,8 @@
 
     i, o = sublanes(384, 512), lanes(384, 512)
     order_in[...] = one_hot((o == (i & 3) * 128 + i // 4) & (i < BLOCK * 4))
-    r = sublanes(256, 256)
-    order_out[...] = one_hot(lanes(256, 256) == (r & 63) // 4 * 16 + r // 64 * 4 + (r & 3))
+    r = sublanes(64, 64)
+    order_out[...] = one_hot(lanes(64, 64) == (r & 15) // 4 * 16 + r // 16 * 4 + (r & 3))
 
     def upwind(buf, r, j, w):
         c = lambda i: cst_ref[s, i : i + 1, j : j + w]
@@ -490,16 +489,10 @@
         total = jnp.sum(part[1, pl.ds(l * POINTS, POINTS), :], axis=1, keepdims=True)
         kept = jnp.where(sublanes(POINTS) == lanes(POINTS), jnp.broadcast_to(total, (POINTS, 128)), 0.0)
         row = jnp.sum(kept, axis=0, keepdims=True)
-        stress[s, b, l : l + 1, :] = row
-        stress[s, b, 4 + l : 5 + l, :] = 0.12 * (east[l] * east[l] + north[l] * north[l]) + 0.02
-    band = [(c, t) for t in peers_b for c in (1 - s, s)] + [(1 - s, b)]
-    rough_copies = []
-    for n, (c, t) in enumerate(band):
-        own_block = stress.at[s, b]
-        rough_copies.append(
-            rcopy(own_block, own_block, r_send.at[n], r_recv.at[s, b], {"comp": c, "ba": t})
-        )
-        rough_copies[-1].start()
+        st[l : l + 1, :] = row
+        st[4 + l : 5 + l, :] = row
+    stress_copy = rcopy(st, st_in, c_send.at[1], c_recv.at[1], partner)
+    stress_copy.start()
 
     energy_copy.wait_recv()
     for l in range(CYCLES):
@@ -521,24 +514,33 @@
     ws_copy = pltpu.make_async_copy(ws_ref, ws_out, o_sem.at[0])
     ws_copy.start()
 
-    for xd in range(1, N_X):
-        for zd in range(N_Z):
-            arrived(lax.rem(x + N_X - xd, N_X) * N_Z + lax.rem(z + zd, N_Z))
-    for k in range(0, 2 * WAVES, 256):
-        gperm[:, k : k + 256] = dot(order_out[...], gath[:, :, k : k + 256].reshape(256, 256)).astype(BF16)
-    for l in range(CYCLES):
-        gw_ref[0, l] = dot(gperm[l * 64 : l * 64 + 64, :], table[l]).astype(BF16)
+    stress_copy.wait_recv()
+    e, n = jnp.concatenate(east * 2, axis=0), jnp.concatenate(north * 2, axis=0)
+    rough[b] = jnp.sqrt(1.0 + 0.03 * (st[...] + st_in[...]) / (0.12 * (e * e + n * n) + 0.02))
+    rough_copies = []
+    for d, t in enumerate(peers_b):
+        rough_copies.append(rcopy(rough.at[b], rough.at[b], r_send.at[d], r_recv.at[b], {"ba": t}))
+        rough_copies[-1].start()
+
+    for xd in (0, 1, 3, 2):
+        col = lax.rem(x + xd, N_X)
+        if xd:
+            for zd in range(N_Z):
+                arrived(col * N_Z + lax.rem(z + zd, N_Z))
+        block = gath[pl.ds(col * N_Z, N_Z)].reshape(64, 2 * WAVES)
+        gperm[...] = dot(order_out[...], block).astype(BF16)
+        for l in range(CYCLES):
+            gw_ref[0, l, pl.ds(pl.multiple_of(col * 16, 16), 16), :] = dot(
+                gperm[l * 16 : l * 16 + 16, :], table[l]
+            ).astype(BF16)
     gw_copy = pltpu.make_async_copy(gw_ref, gw_out, o_sem.at[1])
     gw_copy.start()
 
-    for n, (c, t) in enumerate(band):
-        rcopy(stress.at[c, t], stress.at[c, t], r_send.at[n], r_recv.at[c, t], {"comp": c, "ba": t}).wait_recv()
-    total = stress[0, :, 0:4, :] + stress[1, :, 0:4, :]
-    rough[:, 0:4, :] = jnp.sqrt(1.0 + 0.03 * total / stress[0, :, 4:8, :])
-    rough[:, 4:8, :] = jnp.zeros((N_B, 4, 128), F32)
+    for d, t in enumerate(peers_b):
+        rcopy(rough.at[t], rough.at[t], r_send.at[d], r_recv.at[t], {"ba": t}).wait_recv()
     rough_copy = pltpu.make_async_copy(rough, rough_out, o_sem.at[2])
     rough_copy.start()
-    for c in sent + gathers + rough_copies + [energy_copy]:
+    for c in sent + gathers + rough_copies + [energy_copy, stress_copy]:
         c.wait_send()
     halo_sent(halo_a)
     halo_sent(halo_b)
@@ -622,7 +624,7 @@
             pltpu.VMEM((N_A, 8, 384), F32),
             pltpu.VMEM((N_A, 8, 384), F32),
             pltpu.VMEM((N_B, 16, 2 * WAVES), BF16),
-            pltpu.VMEM((256, 2 * WAVES), BF16),
+            pltpu.VMEM((64, 2 * WAVES), BF16),
             pltpu.VMEM((16, WAVES), F32),
             pltpu.VMEM((16, WAVES), BF16),
             pltpu.VMEM((CYCLES, 2 * WAVES, SLOTS), BF16),
@@ -641,17 +643,18 @@
             pltpu.VMEM((ROWS * COLS, 128), F32),
             pltpu.VMEM((2, ROWS * COLS, 128), F32),
             pltpu.VMEM((ROWS * COLS, 128), F32),
-            pltpu.VMEM((2, N_B, 8, 128), F32),
+            pltpu.VMEM((8, 128), F32),
+            pltpu.VMEM((8, 128), F32),
             pltpu.VMEM((384, 512), BF16),
-            pltpu.VMEM((256, 256), BF16),
+            pltpu.VMEM((64, 64), BF16),
             dma((6,)), dma((GROUPS,)),
             dma((N_A - 1,)), dma((N_A,)),
             dma((N_A,)), dma((N_A,)),
             dma((N_B - 1,)), dma((N_B,)),
             dma((N_B - 1,)), dma((1,)),
             dma((2, 3)), dma((2, 3)),
-            dma((1,)), dma((1,)),
-            dma((2 * N_B - 1,)), dma((2, N_B)),
+            dma((2,)), dma((2,)),
+            dma((N_B - 1,)), dma((N_B,)),
             dma((3,)),
         ],
         compiler_params=pltpu.CompilerParams(

time: 43.8 us -> 43.1 us (0.984)
  Pallas kernels: 43.1 us -> 42.3 us
    pallas_call x1, Pallas kernels: 40.2 us -> 39.4 us  [per_device(): pl.pallas_call(kernel, out_shape=(winds, waves, jax.ShapeDtypeStruct((N_B...]
where the time goes in v9:
time: 43.1 us; the launch traced here: 43 us
  Pallas kernels  42.3 us (98%)
  between operations  0.64 us (1%)
    pallas_call x1, Pallas kernels, per_device(): pl.pallas_call(kernel, out_shape=(winds, waves, jax.ShapeDtypeStruct((N_B...  39.4 us
    pallas_call x1, Pallas kernels, per_device(): pl.pallas_call(last, out_shape=(winds, waves, jax.ShapeDtypeStruct((CYCLE...  2.93 us

profile of v9, /device:TPU:1, one launch (start us, length us, event | category | flops | bytes accessed | tf_op | source)
XLA Modules:
  0.0 43.0 jit_solution(10755504007256501793)
XLA Ops:
  0.6 39.4 %shard_map.103 = (bf16[1,4,64,256]{3,2,1,0:T(8,128)(2,1)}, f32[16,32,648]{2,1,0:T(8,128)}, f32[16,8,128]{2,1,0:T(8,128)}) custom-call(s32[32]{0:T(128)} %cp_hbm.3, bf16[80,32,1280]{2,1,0:T(8,128)(2,1)} %leg_hbm.1, bf16[80,2,4,1280]{3,2,1,0:T(4,128)(2,1)} %bitcast.1, f32[16,32,648]{2,1,0:T(8,128)} %spec_hbm.1, s32[16,32]{1,0:T(8,128)} %mask_hbm.1, ...), custom_call_target="tpu_custom_call" | custom-call | tf_op jit(solution)/shard_map/pallas_call | solution.py:605
  40.0 2.9 %shard_map.104 = (bf16[1,4,64,256]{3,2,1,0:T(8,128)(2,1)}, f32[16,32,648]{2,1,0:T(8,128)}, f32[4,256]{1,0:T(4,128)}) custom-call(s32[32]{0:T(128)} %cp_hbm.3, bf16[1,4,64,256]{3,2,1,0:T(8,128)(2,1)} %get-tuple-element.6.gw_in, f32[16,32,648]{2,1,0:T(8,128)} %get-tuple-element.7.ws_in, f32[16,8,128]{2,1,0:T(8,128)} %get-tuple-element.8.rough_in, s32[4,256]{1,0:T(4,128)} %rs_hbm.1), custom_call_target="tpu_custom_call" | custom-call | tf_op jit(solution)/shard_map/pallas_call | solution.py:667

commit v10 on v9

--- a/solution.py
+++ b/solution.py
@@ -347,7 +347,7 @@
             edge[1, 1, r, :, j : j + w] = v[COLS - 1 : COLS, :]
         return carry
 
-    lax.fori_loop(0, ROWS, second, 0)
+    lax.fori_loop(0, ROWS // 2, lambda r, c: second(2 * r + 1, second(2 * r, c)), 0)
     halo_b = halo(buf_b, 1)
     halo_start(halo_b, buf_b, 1)
 
@@ -418,8 +418,6 @@
     x_peers = [lax.rem(x + d, N_X) * N_Z + z for d in (1, 3, 2)]
     for d in range(1, N_Z):
         give(b, x * N_Z + lax.rem(z + d, N_Z))
-    for t in x_peers:
-        give(b, t)
 
     halo_land(halo_b, buf_b, 1)
 
@@ -438,10 +436,12 @@
                 part[0, at, :w] = total[:, :w] + term
         return carry
 
-    lax.fori_loop(0, ROWS, third, 0)
+    lax.fori_loop(0, ROWS // 2, lambda r, c: third(2 * r + 1, third(2 * r, c)), 0)
     energy_copy = rcopy(part.at[0], part_in, c_send.at[0], c_recv.at[0], partner)
     energy_copy.start()
 
+    for t in x_peers:
+        give(b, t)
     for d in range(1, N_Z):
         o = x * N_Z + lax.rem(z + N_Z - d, N_Z)
         arrived(o)
@@ -484,7 +484,7 @@
                 part[1, at, :w] = total[:, :w] + term
         return carry
 
-    lax.fori_loop(0, ROWS, fourth, 0)
+    lax.fori_loop(0, ROWS // 2, lambda r, c: fourth(2 * r + 1, fourth(2 * r, c)), 0)
     for l in range(CYCLES):
         total = jnp.sum(part[1, pl.ds(l * POINTS, POINTS), :], axis=1, keepdims=True)
         kept = jnp.where(sublanes(POINTS) == lanes(POINTS), jnp.broadcast_to(total, (POINTS, 128)), 0.0)
@@ -510,7 +510,7 @@
             ws_ref[r, :, j : j + w] = (d2[r, :, j : j + w] + grown) / (1.0 + decay)
         return carry
 
-    lax.fori_loop(0, ROWS, fifth, 0)
+    lax.fori_loop(0, ROWS // 2, lambda r, c: fifth(2 * r + 1, fifth(2 * r, c)), 0)
     ws_copy = pltpu.make_async_copy(ws_ref, ws_out, o_sem.at[0])
     ws_copy.start()
 

time: 43.1 us -> 43 us (level)
  no operation moved by 1% of the time
where the time goes in v10:
time: 43 us; the launch traced here: 42.9 us
  Pallas kernels  42.2 us (98%)
  between operations  0.64 us (1%)
    pallas_call x1, Pallas kernels, per_device(): pl.pallas_call(kernel, out_shape=(winds, waves, jax.ShapeDtypeStruct((N_B...  39.3 us
    pallas_call x1, Pallas kernels, per_device(): pl.pallas_call(last, out_shape=(winds, waves, jax.ShapeDtypeStruct((CYCLE...  2.93 us

profile of v10, /device:TPU:1, one launch (start us, length us, event | category | flops | bytes accessed | tf_op | source)
XLA Modules:
  0.0 42.9 jit_solution(12253904722140104690)
XLA Ops:
  0.6 39.3 %shard_map.103 = (bf16[1,4,64,256]{3,2,1,0:T(8,128)(2,1)}, f32[16,32,648]{2,1,0:T(8,128)}, f32[16,8,128]{2,1,0:T(8,128)}) custom-call(s32[32]{0:T(128)} %cp_hbm.3, bf16[80,32,1280]{2,1,0:T(8,128)(2,1)} %leg_hbm.1, bf16[80,2,4,1280]{3,2,1,0:T(4,128)(2,1)} %bitcast.1, f32[16,32,648]{2,1,0:T(8,128)} %spec_hbm.1, s32[16,32]{1,0:T(8,128)} %mask_hbm.1, ...), custom_call_target="tpu_custom_call" | custom-call | tf_op jit(solution)/shard_map/pallas_call | solution.py:605
  39.9 2.9 %shard_map.104 = (bf16[1,4,64,256]{3,2,1,0:T(8,128)(2,1)}, f32[16,32,648]{2,1,0:T(8,128)}, f32[4,256]{1,0:T(4,128)}) custom-call(s32[32]{0:T(128)} %cp_hbm.3, bf16[1,4,64,256]{3,2,1,0:T(8,128)(2,1)} %get-tuple-element.6.gw_in, f32[16,32,648]{2,1,0:T(8,128)} %get-tuple-element.7.ws_in, f32[16,8,128]{2,1,0:T(8,128)} %get-tuple-element.8.rough_in, s32[4,256]{1,0:T(4,128)} %rs_hbm.1), custom_call_target="tpu_custom_call" | custom-call | tf_op jit(solution)/shard_map/pallas_call | solution.py:667
